TPU v7x, 32 devices: a whole 2x2x4 slice. The times are simulated.
32 devices in a mesh: dp: 2 (over y), fsdp: 16 (over z, x, core).
Axes of the slice: x: 2, y: 2, z: 4, core: 2. Of those that a mesh axis runs over, the one named last changes fastest.
Arguments:
- target: bfloat16 [64, 1200, 256], P(('dp', 'fsdp')), may hold values from -6 to 6
- memory: bfloat16 [64, 2048, 256], P(('dp', 'fsdp')), may hold values from -6 to 6
- memory_pos: bfloat16 [64, 2048, 256], P(('dp', 'fsdp')), may hold values from -1 to 1
- segment: int32 [64, 2048], P(('dp', 'fsdp')), may hold values from 0 to 12, as said below
- project_weight: bfloat16 [6, 256, 256], P(None, ('dp', 'fsdp')), may hold values from -0.375 to 0.375
- output_weight: bfloat16 [2, 256, 256], P(None, ('dp', 'fsdp')), may hold values from -1 to 1
- expand_weight: bfloat16 [256, 2048], P(None, ('dp', 'fsdp')), may hold values from -0.375 to 0.375
- shrink_weight: bfloat16 [2048, 256], P(('dp', 'fsdp')), may hold values from -0.125 to 0.125
- box_weight: bfloat16 [2, 256, 256], P(None, ('dp', 'fsdp')), may hold values from -0.375 to 0.375
- class_weight: bfloat16 [256, 92], P(('dp', 'fsdp')), may hold values from -0.375 to 0.375
- box_final: bfloat16 [256, 4], P(('dp', 'fsdp')), may hold values from -0.375 to 0.375
- query_pos: bfloat16 [100, 256], P(None, ('dp', 'fsdp')), may hold values from -6 to 6
- norm_gains: bfloat16 [4, 256], P(None, ('dp', 'fsdp')), may hold values from 0.25 to 1.75
- biases: bfloat16 [13, 256], P(None, ('dp', 'fsdp')), may hold values from -4 to 4
- expand_bias: bfloat16 [2048], P(('dp', 'fsdp')), may hold values from -4 to 4
- head_bias: bfloat16 [96], replicated, may hold values from -6 to 6
- output_cotangent: bfloat16 [64, 1200, 256], P(('dp', 'fsdp')), may hold values from -6 to 6
- logit_cotangent: bfloat16 [64, 1200, 92], P(('dp', 'fsdp')), may hold values from -6 to 6
- box_cotangent: bfloat16 [64, 1200, 4], P(('dp', 'fsdp')), may hold values from -6 to 6
Outputs:
- layer_output: bfloat16 [64, 1200, 256], P(('dp', 'fsdp'))
- target_grad: float32 [64, 1200, 256], P(('dp', 'fsdp'))
- memory_grad: float32 [64, 2048, 256], P(('dp', 'fsdp'))
- project_grad: float32 [6, 256, 256], P(None, ('dp', 'fsdp'))
- output_grad: float32 [2, 256, 256], P(None, ('dp', 'fsdp'))
- expand_grad: float32 [256, 2048], P(None, ('dp', 'fsdp'))
- shrink_grad: float32 [2048, 256], P(('dp', 'fsdp'))
- box_weight_grad: float32 [2, 256, 256], P(None, ('dp', 'fsdp'))
- class_grad: float32 [256, 92], P(('dp', 'fsdp'))
- box_final_grad: float32 [256, 4], P(('dp', 'fsdp'))
- query_pos_grad: float32 [100, 256], P(None, ('dp', 'fsdp'))
- gains_grad: float32 [4, 256], P(None, ('dp', 'fsdp'))
- biases_grad: float32 [13, 256], P(None, ('dp', 'fsdp'))
- expand_bias_grad: float32 [2048], P(('dp', 'fsdp'))
- head_bias_grad: float32 [96], replicated
Inputs may be any that keep to these rules, and one draw needn't show every extreme that they name: `segment`: in each pack the images are contiguous non-empty runs of tokens numbered 0, 1, 2 in order, a pack holds 6 to 12 images, its last one or more tokens are padding marked 12, and some pack holds 12 images.
All inputs are finite; a program needn't handle non-finite values.
Results may differ from a plain program's by a relative error of at most 0.018.
The roundings to bfloat16 on the way count: a program that leaves them out, or rounds other values in their place, can miss the bound.
Values may be sent and summed in bfloat16 or wider, within the bound.
No kernel may reach another device: no remote copies, remote signals or barrier semaphores. Data moves between devices by JAX's collectives and lax.ppermute only.
A program may use at most 576 MiB of HBM per device.

v0:
```python
import functools

import jax
import jax.numpy as jnp
from jax import lax
from jax.experimental import pallas as pl
from jax.experimental.pallas import tpu as pltpu
from jax.sharding import PartitionSpec as P

D = 256
HEADS = 8
NQ = 100
CLS = 92
IMG_MAX = 12
HEAD_DIM = 32
QP = 128
ROWS = IMG_MAX * QP
PAIRS = HEADS // 2
BLOCK = 256
SIZES = (128, 192, 256, 384, 512)
SHORT = (128, 192, 256, 512)
CHUNK = 512
STEP = 400
FF_BLOCKS = 8
GAIN = 96
BIAS = 100
POS = 128
SMALL = 8
EXTRA = 16
ME = 14

epsilon = 1e-05
masked = -1000000000.0
scale = HEAD_DIM ** (-0.5)
log2e = 1.4426950408889634
gelu_a = 0.7978845608028654
gelu_b = gelu_a * 0.044715
AXES = ("dp", "fsdp")
f32 = jnp.float32
bf16 = jnp.bfloat16


def nn(left, right):
    return jnp.dot(left, right, preferred_element_type=f32)


def nt(left, right):
    return lax.dot_general(left, right, (((1,), (1,)), ((), ())), preferred_element_type=f32)


def tn(left, right):
    return lax.dot_general(left, right, (((0,), (0,)), ((), ())), preferred_element_type=f32)


def total(value):
    return jnp.sum(value, axis=0, keepdims=True)


def norm_parts(value):
    middle = jnp.mean(value, axis=-1, keepdims=True)
    centered = value - middle
    spread = jnp.mean(centered * centered, axis=-1, keepdims=True)
    inverse = lax.rsqrt(spread + epsilon)
    return centered * inverse, inverse


def norm_back(unit, inverse, gain, grad):
    scaled = grad * gain
    first = jnp.mean(scaled, axis=-1, keepdims=True)
    second = jnp.mean(scaled * unit, axis=-1, keepdims=True)
    return inverse * (scaled - first - unit * second)


def gelu_parts(value):
    square = value * value
    cdf = 0.5 + 0.5 * jnp.tanh(value * (gelu_a + gelu_b * square))
    result = value * cdf
    slope = cdf + (result - result * cdf) * (2.0 * gelu_a + 6.0 * gelu_b * square)
    return result, slope


def spread_heads(value, spread_ref):
    lane = lax.broadcasted_iota(jnp.int32, (1, D), 1) // HEAD_DIM
    for head in range(HEADS):
        keep = (lane == head).astype(f32).astype(bf16)
        spread_ref[head * QP : (head + 1) * QP, :] = value * keep


def pair_rows(ref, pair):
    side = pair // 2 * (D // 2)
    return ref[2 * QP * pair : 2 * QP * (pair + 1), side : side + D // 2]


def long_rows(ref, pair):
    return ref[2 * QP * pair : 2 * QP * (pair + 1), :]


def head_lane(lanes):
    return lax.broadcasted_iota(jnp.int32, (1, lanes), 1) // HEAD_DIM


def join_pairs(products):
    lane = head_lane(D)
    result = products[0][:QP]
    for head in range(1, HEADS):
        part = products[head // 2][(head % 2) * QP : (head % 2 + 1) * QP]
        result = jnp.where(lane == head, part, result)
    return result


def join_halves(products):
    lane = head_lane(D // 2)
    halves = []
    for half in range(2):
        low, high = products[2 * half : 2 * half + 2]
        part = jnp.where(lane == 2, high[:QP], high[QP:])
        part = jnp.where(lane == 1, low[QP:], part)
        halves.append(jnp.where(lane == 0, low[:QP], part))
    return jnp.concatenate(halves, axis=1)


def half_lanes(value, pair):
    side = pair // 2 * (D // 2)
    return value[:, side : side + D // 2]


def row_loop(size, step):
    def run(body):
        @pl.loop(0, size // step)
        def _(index):
            start = pl.multiple_of(index * step, step)
            body(start, pl.ds(start, step))

    return run


def chunk_loop(size, step):
    def run(body):
        for start in range(0, size, step):
            body(start, slice(start, start + step))

    return run


def attend_block(key, value, spread_ref, valid, halves):
    scores = [nt(half_lanes(key, pair), pair_rows(spread_ref, pair)) for pair in range(PAIRS)]
    attends = []
    logs = []
    for pair in range(PAIRS):
        kept = jnp.where(valid, scores[pair], masked)
        top = jnp.max(kept, axis=0, keepdims=True)
        raised = jnp.exp2((kept - top) * (scale * log2e))
        sums = total(raised)
        attends.append((raised * (1.0 / sums)).astype(bf16))
        logs.append(top * (scale * log2e) + jnp.log2(sums))
    if halves:
        products = [tn(attends[pair], half_lanes(value, pair)) for pair in range(PAIRS)]
        context = join_halves(products)
    else:
        context = join_pairs([tn(attends[pair], value) for pair in range(PAIRS)])
    return context, jnp.concatenate(logs, axis=1)


def place_of(device, bounds, ordered, parts):
    return order_of(device ^ bounds[0, ME], parts) if ordered else device


def early_self_kernel(
    ordered,
    bounds,
    target_ref,
    memory_ref,
    pos_ref,
    mine_ref,
    other_ref,
    after_ref,
    qs_ref,
    ks_ref,
    vs_ref,
    cs_ref,
    inner_ref,
    cq_ref,
    ck_ref,
    cv_ref,
    mean_ref,
    w_ref,
    small_ref,
    flat_ref,
    rows_ref,
    spread_ref,
    block_ref,
    unit_ref,
):
    pack = pl.program_id(0)
    slots = target_ref.shape[1]
    tokens = memory_ref.shape[1]
    near = mine_ref.shape[0]
    parts = 2 * near
    share = D // parts

    @pl.when(pack == 0)
    def _():
        block_ref[0:near] = mine_ref[...]
        block_ref[near:] = other_ref[...]

        @pl.loop(0, parts)
        def _(device):
            block = block_ref[place_of(device, bounds, ordered, parts)].astype(f32)
            rows = pl.ds(pl.multiple_of(device * share, share), share)
            for unit in range(SMALL + 1):
                unit_ref[unit, rows, :] = block[unit * share : (unit + 1) * share]

        w_ref[...] = unit_ref[...].astype(bf16)
        small_ref[...] = unit_ref[SMALL].T

    def bias(index):
        return small_ref[BIAS + index : BIAS + index + 1, :]

    def gain(index):
        return small_ref[GAIN + index : GAIN + index + 1, :]

    inside = lax.broadcasted_iota(jnp.int32, (QP, 1), 0) < NQ
    position = small_ref[POS : POS + QP, :]
    positions = jnp.concatenate([position] * (CHUNK // QP), axis=0)

    mean_ref[0] = jnp.zeros((1, D), f32)
    @chunk_loop(tokens, CHUNK)
    def _(start, rows):
        memory = memory_ref[0, rows, :]
        joined = (memory.astype(f32) + pos_ref[0, rows, :].astype(f32)).astype(bf16)
        ck_ref[0, rows, :] = nn(joined, w_ref[4]).astype(bf16)
        value = (nn(memory, w_ref[5]) + bias(4)).astype(bf16)
        cv_ref[0, rows, :] = value
        mean_ref[0] += total(value.astype(f32)) * (1.0 / tokens)

    flat_ref[0:slots, :] = target_ref[0].astype(f32)
    for image in range(IMG_MAX):
        part = flat_ref[image * NQ : image * NQ + QP, :]
        rows_ref[image * QP : (image + 1) * QP, :] = jnp.where(inside, part, 0.0)

    @chunk_loop(ROWS, CHUNK)
    def _(start, rows):
        target = rows_ref[rows, :]
        joined = (target + positions).astype(bf16)
        qs_ref[0, rows, :] = (nn(joined, w_ref[0]) + bias(0)).astype(bf16)
        ks_ref[0, rows, :] = nn(joined, w_ref[1]).astype(bf16)
        vs_ref[0, rows, :] = (nn(target.astype(bf16), w_ref[2]) + bias(1)).astype(bf16)

    @pl.loop(0, IMG_MAX // 2)
    def _(step):
        for turn in range(2):
            rows = pl.ds(pl.multiple_of((2 * step + turn) * QP, QP), QP)
            spread = spread_ref.at[turn]
            spread_heads(qs_ref[0, rows, :], spread)
            context, unused = attend_block(
                ks_ref[0, rows, :], vs_ref[0, rows, :], spread, inside, True
            )
            cs_ref[0, rows, :] = context.astype(bf16)

    @chunk_loop(ROWS, CHUNK)
    def _(start, rows):
        value = rows_ref[rows, :] + nn(cs_ref[0, rows, :], w_ref[6]) + bias(2)
        inner_ref[0, rows, :] = value
        unit, unused = norm_parts(value)
        after = unit * gain(0) + bias(9)
        after_ref[0, rows, :] = after
        query = nn((after + positions).astype(bf16), w_ref[3]) + bias(3)
        cq_ref[0, rows, :] = query.astype(bf16)


def early_cross_kernel(
    bounds,
    rows_in_ref,
    cq_ref,
    ck_ref,
    cv_ref,
    mean_ref,
    w_ref,
    small_in_ref,
    after_ref,
    cc_ref,
    log_ref,
    rows_ref,
    spread_ref,
    score_ref,
    top_ref,
    sum_ref,
    out_ref,
    bias_ref,
):
    pack = pl.program_id(0)
    tokens = ck_ref.shape[1]

    @pl.when(pack == 0)
    def _():
        bias_ref[...] = small_in_ref[0].astype(f32).T[BIAS + 5 : BIAS + 6]

    @pl.loop(0, IMG_MAX)
    def _(image):
        rows = pl.ds(pl.multiple_of(image * QP, QP), QP)
        first = bounds[pack, image]
        last = bounds[pack, image + 1]
        origin = (first // 16) * 16
        blocks = (last - origin + (BLOCK - 1)) // BLOCK
        spread = spread_ref
        spread_heads(cq_ref[0, rows, :], spread)

        def place_at(block, size=BLOCK):
            wanted = origin + block * size
            start = pl.multiple_of(jnp.minimum(wanted, tokens - size), 16)
            token = start + lax.broadcasted_iota(jnp.int32, (size, 1), 0)
            valid = (token >= jnp.maximum(first, wanted)) & (token < last)
            return pl.ds(start, size), valid

        def fits(index):
            below = SHORT[index - 1] if index else 0
            return (last > first) & (last - origin > below) & (last - origin <= SHORT[index])

        @pl.when(last == first)
        def _():
            cc_ref[0, rows, :] = jnp.broadcast_to(mean_ref[0], (QP, D)).astype(bf16)
            log_ref[0, image] = jnp.zeros((1, HEADS * QP), f32)

        def in_one(size):
            place, valid = place_at(0, size)
            context, logs = attend_block(
                ck_ref[0, place, :], cv_ref[0, place, :], spread, valid, False
            )
            cc_ref[0, rows, :] = context.astype(bf16)
            log_ref[0, image] = logs

        for index, size in enumerate(SHORT):
            pl.when(fits(index))(functools.partial(in_one, size))

        @pl.when(last - origin > SHORT[-1])
        def _():
            top_ref[...] = jnp.full_like(top_ref, masked)
            sum_ref[...] = jnp.zeros_like(sum_ref)
            out_ref[...] = jnp.zeros_like(out_ref)

            @pl.loop(0, blocks)
            def _(block):
                place, valid = place_at(block)
                kept = pl.ds(pl.multiple_of(block * BLOCK, BLOCK), BLOCK)
                key = ck_ref[0, place, :]
                for pair in range(PAIRS):
                    lanes = slice(2 * QP * pair, 2 * QP * (pair + 1))
                    scores = jnp.where(valid, nt(key, long_rows(spread, pair)), masked)
                    score_ref[kept, lanes] = scores
                    top = jnp.max(scores, axis=0, keepdims=True)
                    top_ref[:, lanes] = jnp.maximum(top_ref[:, lanes], top)

            @pl.loop(0, blocks)
            def _(block):
                kept = pl.ds(pl.multiple_of(block * BLOCK, BLOCK), BLOCK)
                raised = jnp.exp2((score_ref[kept, :] - top_ref[...]) * (scale * log2e))
                score_ref[kept, :] = raised
                sum_ref[...] += total(raised)

            @pl.loop(0, blocks)
            def _(block):
                place, unused = place_at(block)
                kept = pl.ds(pl.multiple_of(block * BLOCK, BLOCK), BLOCK)
                value = cv_ref[0, place, :]
                products = []
                for pair in range(PAIRS):
                    lanes = slice(2 * QP * pair, 2 * QP * (pair + 1))
                    attend = (score_ref[kept, lanes] * (1.0 / sum_ref[:, lanes])).astype(bf16)
                    products.append(tn(attend, value))
                out_ref[...] += join_pairs(products)

            cc_ref[0, rows, :] = out_ref[...].astype(bf16)
            log_ref[0, image] = top_ref[...] * (scale * log2e) + jnp.log2(sum_ref[...])

    @chunk_loop(ROWS, CHUNK)
    def _(start, rows):
        rows_ref[rows, :] = rows_in_ref[0, rows, :] + nn(cc_ref[0, rows, :], w_ref[0]) + bias_ref[...]
    for image in range(IMG_MAX):
        after_ref[0, image * NQ : (image + 1) * NQ, :] = rows_ref[image * QP : image * QP + NQ, :]


def lanes_of(count, first, lanes=POS):
    row = lax.broadcasted_iota(jnp.int32, (count, lanes), 0)
    lane = lax.broadcasted_iota(jnp.int32, (count, lanes), 1)
    return (row + first == lane).astype(f32).astype(bf16)


def middle_kernel(
    ordered,
    bounds,
    x_ref,
    cot_ref,
    head_cot_ref,
    mine_ref,
    other_ref,
    small_in_ref,
    head_bias_ref,
    layer_ref,
    grad_ref,
    keep_ref,
    send_ref,
    dhead_ref,
    drow_ref,
    small_ref,
    bias_ref,
    box_ref,
    low_ref,
    cross_ref,
    sum_ref,
    branch_ref,
    hidden_ref,
    slope_ref,
    ff_ref,
    dff_ref,
    unit_ref,
):
    pack = pl.program_id(0)
    slots = x_ref.shape[1]
    half = mine_ref.shape[0]
    parts = 2 * half
    ff = FF_BLOCKS * D // parts
    share = D // parts
    near = D // ff
    boxes = 2 * ff
    extra = 2 * ff + 2 * share

    @pl.when(pack == 0)
    def _():
        small_ref[...] = small_in_ref[0].astype(f32).T
        ff_ref[0:half] = mine_ref[...]
        ff_ref[half:] = other_ref[...]

        @pl.loop(0, parts)
        def _(device):
            place = place_of(device, bounds, ordered, parts)
            pair = ff_ref[place, boxes:extra, :].astype(f32)
            rows = pl.ds(pl.multiple_of(device * share, share), share)
            unit_ref[0, rows, :] = pair[:share]
            unit_ref[1, rows, :] = pair[share:]

        box_ref[...] = unit_ref[...].astype(bf16)
        unit_ref[...] = jnp.zeros_like(unit_ref)
        for block in range(FF_BLOCKS):
            rows = [ff_ref[block * near + k, extra : extra + 16, :] for k in range(near)]
            rows = [row.astype(f32)[1:2, 0:ff] for row in rows]
            bias_ref[block] = jnp.concatenate(rows, axis=1)
        bias_ref[FF_BLOCKS:] = jnp.zeros((FF_BLOCKS, 1, D), f32)
        dff_ref[...] = jnp.zeros_like(dff_ref)
        dhead_ref[...] = jnp.zeros_like(dhead_ref)
        drow_ref[...] = jnp.zeros_like(drow_ref)

    def bias(index):
        return small_ref[BIAS + index : BIAS + index + 1, :]

    def gain(index):
        return small_ref[GAIN + index : GAIN + index + 1, :]

    def add_row(column, value):
        row = column - GAIN
        drow_ref[row : row + 1, :] += value

    def near_block(block):
        return pl.ds(block * near, near)

    def shrink(block):
        return ff_ref[near_block(block), 0:ff, :].reshape(D, D)

    def expand(block):
        return ff_ref[near_block(block), ff:boxes, :].reshape(D, D)

    @row_loop(slots, STEP)
    def _(start, rows):
        unit, unused = norm_parts(x_ref[0, rows, :])
        after_cross = unit * gain(1) + bias(10)
        cross_ref[rows, :] = after_cross
        low_ref[rows, :] = after_cross.astype(bf16)

    sum_ref[...] = cross_ref[...] + bias(6)
    hidden_ref[FF_BLOCKS - 1] = jnp.zeros((slots, D), bf16)

    @pl.loop(0, FF_BLOCKS)
    def _(block):
        before = (block + FF_BLOCKS - 1) % FF_BLOCKS
        sum_ref[...] += nn(hidden_ref[before], shrink(before))
        value, slope = gelu_parts(nt(low_ref[...], expand(block)) + bias_ref[block])
        hidden_ref[block] = value.astype(bf16)
        slope_ref[block] = slope

    sum_ref[...] += nn(hidden_ref[FF_BLOCKS - 1], shrink(FF_BLOCKS - 1))

    head_weight = small_in_ref[0, :, 0:POS]
    lane = lax.broadcasted_iota(jnp.int32, (1, POS), 1)
    is_box = (lane >= CLS) & (lane < CLS + 4)
    @chunk_loop(slots, STEP)
    def _(start, rows):
        slot = start + lax.broadcasted_iota(jnp.int32, (STEP, 1), 0)
        live = (slot < bounds[pack, IMG_MAX + 1] * NQ).astype(f32)
        unit_ffn, inverse_ffn = norm_parts(sum_ref[rows, :])
        after_ffn = unit_ffn * gain(2) + bias(11)
        layer_ref[0, rows, :] = (after_ffn * live).astype(bf16)
        unit_last, inverse_last = norm_parts(after_ffn)
        normed = (unit_last * gain(3) + bias(12)).astype(bf16)
        one, one_slope = gelu_parts(nn(normed, box_ref[0]) + bias(7))
        box_one = one.astype(bf16)
        two, two_slope = gelu_parts(nn(box_one, box_ref[1]) + bias(8))
        box_two = two.astype(bf16)
        box = jax.nn.sigmoid(nn(box_two, head_weight) + head_bias_ref[0:1, :])

        head_cot = head_cot_ref[0, rows, :].astype(f32) * live
        grad_box = jnp.where(is_box, head_cot * box * (1.0 - box), 0.0).astype(bf16)
        grad_logit = jnp.where(lane < CLS, head_cot, 0.0).astype(bf16)
        drow_ref[31:32, 0:POS] += total(grad_box.astype(f32)) + total(grad_logit.astype(f32))
        normed_t = normed.T
        grad_two = (two_slope * nt(grad_box, head_weight)).astype(bf16)
        grad_one = (one_slope * nt(grad_two, box_ref[1])).astype(bf16)
        dhead_ref[...] += nn(normed_t, grad_logit) + tn(box_two, grad_box)
        unit_ref[0] += nn(normed_t, grad_one)
        unit_ref[1] += tn(box_one, grad_two)
        add_row(BIAS + 8, total(grad_two.astype(f32)))
        add_row(BIAS + 7, total(grad_one.astype(f32)))
        grad_normed = nt(grad_one, box_ref[0]) + nt(grad_logit, head_weight)
        add_row(GAIN + 3, total(grad_normed * unit_last))
        add_row(BIAS + 12, total(grad_normed))
        grad_after = cot_ref[0, rows, :].astype(f32) * live + norm_back(
            unit_last, inverse_last, gain(3), grad_normed
        )
        add_row(GAIN + 2, total(grad_after * unit_ffn))
        add_row(BIAS + 11, total(grad_after))
        grad_ffn = norm_back(unit_ffn, inverse_ffn, gain(2), grad_after)
        grad_branch = grad_ffn.astype(bf16)
        add_row(BIAS + 6, total(grad_branch.astype(f32)))
        sum_ref[rows, :] = grad_ffn
        branch_ref[rows, :] = grad_branch

    @pl.loop(0, FF_BLOCKS)
    def _(block):
        branch = branch_ref[...]
        dpre = (nt(branch, shrink(block)) * slope_ref[block]).astype(bf16)
        bias_ref[FF_BLOCKS + block] += total(dpre.astype(f32))
        dshrink = tn(hidden_ref[block], branch).reshape(near, ff, D)
        dff_ref[near_block(block), 0:ff, :] += dshrink
        dexpand = tn(dpre, low_ref[...]).reshape(near, ff, D)
        dff_ref[near_block(block), ff:boxes, :] += dexpand
        sum_ref[...] += nn(dpre, expand(block))

    @row_loop(slots, STEP)
    def _(start, rows):
        unit, inverse = norm_parts(x_ref[0, rows, :])
        grad = sum_ref[rows, :]
        add_row(GAIN + 1, total(grad * unit))
        add_row(BIAS + 10, total(grad))
        grad_ref[0, rows, :] = norm_back(unit, inverse, gain(1), grad)

    @pl.when(pack == pl.num_programs(0) - 1)
    def _():
        @pl.loop(0, parts)
        def _(device):
            place = place_of(device, bounds, ordered, parts)
            rows = pl.ds(pl.multiple_of(device * share, share), share)
            dff_ref[place, boxes : boxes + share, :] = unit_ref[0, rows, :]
            dff_ref[place, boxes + share : extra, :] = unit_ref[1, rows, :]

        for part in range(parts):
            dff_ref[part, extra : extra + 1, :] = drow_ref[31:32, :]
            side = part % near * ff
            values = bias_ref[FF_BLOCKS + part // near][:, side : side + ff]
            dff_ref[part, extra + 1 : extra + 2, 0:ff] = values
        keep_ref[...] = dff_ref[0:half]
        send_ref[...] = dff_ref[half:].astype(bf16)


def attend_back(key, value, spread, spread_grad, valid, logs, attend_ref, score_ref):
    scores = [nt(half_lanes(key, pair), pair_rows(spread, pair)) for pair in range(PAIRS)]
    grads = [nt(half_lanes(value, pair), pair_rows(spread_grad, pair)) for pair in range(PAIRS)]
    lows = []
    for pair in range(PAIRS):
        lanes = slice(2 * QP * pair, 2 * QP * (pair + 1))
        if logs is None:
            kept = jnp.where(valid, scores[pair], masked)
            top = jnp.max(kept, axis=0, keepdims=True)
            raised = jnp.exp2((kept - top) * (scale * log2e))
            attend = raised * (1.0 / total(raised))
        else:
            attend = jnp.exp2(scores[pair] * (scale * log2e) - logs[:, lanes])
            attend = jnp.where(valid, attend, 0.0)
        row_dot = total(attend * grads[pair])
        low = (attend * (grads[pair] - row_dot)).astype(bf16)
        attend_ref[:, lanes] = attend.astype(bf16)
        score_ref[:, lanes] = low
        lows.append(low)
    return join_halves([tn(lows[pair], half_lanes(key, pair)) for pair in range(PAIRS)]) * scale


def late_cross_kernel(
    bounds,
    grad_ref,
    memory_ref,
    pos_ref,
    w_ref,
    cq_ref,
    ck_ref,
    cv_ref,
    cc_ref,
    log_ref,
    gq_ref,
    dmemory_ref,
    dw_ref,
    drows_ref,
    flat_ref,
    grad_rows_ref,
    context_ref,
    dv_ref,
    spread_ref,
    spread_grad_ref,
    attend_ref,
    score_ref,
    sum_ref,
    out_ref,
):
    pack = pl.program_id(0)
    slots = grad_ref.shape[1]
    tokens = memory_ref.shape[1]

    @pl.when(pack == 0)
    def _():
        dw_ref[...] = jnp.zeros_like(dw_ref)
        drows_ref[...] = jnp.zeros_like(drows_ref)

    def add_row(row, value):
        drows_ref[row : row + 1, :] += value

    inside = lax.broadcasted_iota(jnp.int32, (QP, 1), 0) < NQ

    flat_ref[0:slots, :] = grad_ref[0]
    for image in range(IMG_MAX):
        part = flat_ref[image * NQ : image * NQ + QP, :]
        grad_rows_ref[image * QP : (image + 1) * QP, :] = jnp.where(inside, part, 0.0)
    @chunk_loop(ROWS, CHUNK)
    def _(start, rows):
        branch = grad_rows_ref[rows, :].astype(bf16)
        add_row(1, total(branch.astype(f32)))
        dw_ref[2] += tn(cc_ref[0, rows, :], branch)
        context_ref[rows, :] = nt(branch, w_ref[7]).astype(bf16)
    dmemory_ref[...] = jnp.zeros_like(dmemory_ref)
    dv_ref[...] = jnp.zeros_like(dv_ref)

    @pl.loop(0, IMG_MAX)
    def _(image):
        rows = pl.ds(pl.multiple_of(image * QP, QP), QP)
        first = bounds[pack, image]
        last = bounds[pack, image + 1]
        origin = (first // 16) * 16
        blocks = (last - origin + (BLOCK - 1)) // BLOCK
        spread = spread_ref
        spread_grad = spread_grad_ref
        attend_low = attend_ref
        score_low = score_ref
        spread_heads(cq_ref[0, rows, :], spread)
        spread_heads(context_ref[rows, :], spread_grad)
        logs = log_ref[0, image]

        def place_at(block, size=BLOCK):
            wanted = origin + block * size
            start = pl.multiple_of(jnp.minimum(wanted, tokens - size), 16)
            token = start + lax.broadcasted_iota(jnp.int32, (size, 1), 0)
            valid = (token >= jnp.maximum(first, wanted)) & (token < last)
            return pl.ds(start, size), valid

        def fits(index):
            below = SIZES[index - 1] if index else 0
            return (last > first) & (last - origin > below) & (last - origin <= SIZES[index])

        @pl.when(last == first)
        def _():
            gq_ref[0, rows, :] = jnp.zeros((QP, D), bf16)

        def in_one(size):
            place, valid = place_at(0, size)
            attend_part = attend_low.at[0:size]
            score_part = score_low.at[0:size]
            grad_query = attend_back(
                ck_ref[0, place, :],
                cv_ref[0, place, :],
                spread,
                spread_grad,
                valid,
                logs,
                attend_part,
                score_part,
            )
            gq_ref[0, rows, :] = grad_query.astype(bf16)
            dv_ref[place, :] += nn(attend_part[...], spread_grad[...])
            dmemory_ref[0, place, :] += nn(score_part[...], spread[...])

        for index, size in enumerate(SIZES):
            pl.when(fits(index))(functools.partial(in_one, size))

        @pl.when(last - origin > SIZES[-1])
        def _():
            sum_ref[...] = jnp.zeros_like(sum_ref)
            out_ref[...] = jnp.zeros_like(out_ref)

            @pl.loop(0, blocks)
            def _(block):
                place, valid = place_at(block)
                for pair in range(PAIRS):
                    lanes = slice(2 * QP * pair, 2 * QP * (pair + 1))
                    scores = nt(ck_ref[0, place, :], long_rows(spread, pair))
                    attend = jnp.exp2(scores * (scale * log2e) - logs[:, lanes])
                    attend = jnp.where(valid, attend, 0.0)
                    grad_attend = nt(cv_ref[0, place, :], long_rows(spread_grad, pair))
                    sum_ref[:, lanes] += total(attend * grad_attend)

            @pl.loop(0, blocks)
            def _(block):
                place, valid = place_at(block)
                key = ck_ref[0, place, :]
                products = []
                for pair in range(PAIRS):
                    lanes = slice(2 * QP * pair, 2 * QP * (pair + 1))
                    scores = nt(ck_ref[0, place, :], long_rows(spread, pair))
                    attend = jnp.exp2(scores * (scale * log2e) - logs[:, lanes])
                    attend = jnp.where(valid, attend, 0.0)
                    grad_attend = nt(cv_ref[0, place, :], long_rows(spread_grad, pair))
                    grad_scores = attend * (grad_attend - sum_ref[:, lanes])
                    grad_scores = grad_scores.astype(bf16)
                    attend_low[0:BLOCK, lanes] = attend.astype(bf16)
                    score_low[0:BLOCK, lanes] = grad_scores
                    products.append(tn(grad_scores, half_lanes(key, pair)))
                out_ref[...] += join_halves(products)
                dv_ref[place, :] += nn(attend_low[0:BLOCK, :], spread_grad[...])
                dmemory_ref[0, place, :] += nn(score_low[0:BLOCK, :], spread[...])

            gq_ref[0, rows, :] = (out_ref[...] * scale).astype(bf16)

    @chunk_loop(tokens, CHUNK)
    def _(start, rows):
        memory = memory_ref[0, rows, :]
        joined = (memory.astype(f32) + pos_ref[0, rows, :].astype(f32)).astype(bf16)
        grad_key = (dmemory_ref[0, rows, :] * scale).astype(bf16)
        grad_value = dv_ref[rows, :].astype(bf16)
        dmemory_ref[0, rows, :] = nt(grad_key, w_ref[4]) + nt(grad_value, w_ref[5])
        add_row(0, total(grad_value.astype(f32)))
        dw_ref[0] += tn(joined, grad_key)
        dw_ref[1] += tn(memory, grad_value)


def late_self_kernel(
    ordered,
    bounds,
    grad_ref,
    gcq_ref,
    target_ref,
    w_ref,
    qs_ref,
    ks_ref,
    vs_ref,
    cs_ref,
    inner_ref,
    dcross_ref,
    dcross_rows_ref,
    dhead_ref,
    drow_ref,
    dtarget_ref,
    keep_ref,
    send_ref,
    small_ref,
    flat_ref,
    grad_rows_ref,
    place_ref,
    context_ref,
    gq_ref,
    gk_ref,
    gv_ref,
    spread_ref,
    spread_grad_ref,
    attend_ref,
    score_ref,
    drows_ref,
    dw_ref,
    block_ref,
):
    pack = pl.program_id(0)
    slots = target_ref.shape[1]

    @pl.when(pack == 0)
    def _():
        small_ref[...] = w_ref[SMALL].astype(f32).T
        dw_ref[0:4] = jnp.zeros((4, D, D), f32)
        dw_ref[4:6] = dcross_ref[0:2]
        dw_ref[6] = jnp.zeros((D, D), f32)
        dw_ref[7] = dcross_ref[2]
        drows_ref[...] = jnp.zeros_like(drows_ref)
        drows_ref[GAIN : GAIN + 32, :] = drow_ref[...]
        drows_ref[BIAS + 4 : BIAS + 6, :] += dcross_rows_ref[0:2, :]

    def bias(index):
        return small_ref[BIAS + index : BIAS + index + 1, :]

    def gain(index):
        return small_ref[GAIN + index : GAIN + index + 1, :]

    def add_row(row, value):
        drows_ref[row : row + 1, :] += value

    inside = lax.broadcasted_iota(jnp.int32, (QP, 1), 0) < NQ
    position = small_ref[POS : POS + QP, :]
    positions = jnp.concatenate([position] * (CHUNK // QP), axis=0)

    flat_ref[0:slots, :] = grad_ref[0]
    for image in range(IMG_MAX):
        part = flat_ref[image * NQ : image * NQ + QP, :]
        grad_rows_ref[image * QP : (image + 1) * QP, :] = jnp.where(inside, part, 0.0)
    flat_ref[0:slots, :] = target_ref[0].astype(f32)

    @chunk_loop(ROWS, CHUNK)
    def _(start, rows):
        unit, inverse = norm_parts(inner_ref[0, rows, :])
        cross_in = (unit * gain(0) + bias(9) + positions).astype(bf16)
        grad_query = gcq_ref[0, rows, :]
        add_row(BIAS + 3, total(grad_query.astype(f32)))
        dw_ref[3] += tn(cross_in, grad_query)
        place = nt(grad_query, w_ref[3])
        place_ref[rows, :] = place
        grad = grad_rows_ref[rows, :] + place
        add_row(GAIN, total(grad * unit))
        add_row(BIAS + 9, total(grad))
        grad = norm_back(unit, inverse, gain(0), grad)
        grad_rows_ref[rows, :] = grad
        branch = grad.astype(bf16)
        add_row(BIAS + 2, total(branch.astype(f32)))
        dw_ref[6] += tn(cs_ref[0, rows, :], branch)
        context_ref[rows, :] = nt(branch, w_ref[6]).astype(bf16)

    @pl.loop(0, IMG_MAX // 2)
    def _(step):
        for turn in range(2):
            rows = pl.ds(pl.multiple_of((2 * step + turn) * QP, QP), QP)
            spread = spread_ref.at[turn]
            spread_grad = spread_grad_ref.at[turn]
            attend_low = attend_ref.at[turn * QP : (turn + 1) * QP]
            score_low = score_ref.at[turn * QP : (turn + 1) * QP]
            spread_heads(qs_ref[0, rows, :], spread)
            spread_heads(context_ref[rows, :], spread_grad)
            grad_query = attend_back(
                ks_ref[0, rows, :],
                vs_ref[0, rows, :],
                spread,
                spread_grad,
                inside,
                None,
                attend_low,
                score_low,
            )
            gq_ref[rows, :] = grad_query.astype(bf16)
            gv_ref[rows, :] = nn(attend_low[...], spread_grad[...]).astype(bf16)
            gk_ref[rows, :] = (nn(score_low[...], spread[...]) * scale).astype(bf16)

    for start in range(0, ROWS, CHUNK):
        rows = slice(start, start + CHUNK)
        images = range(start // QP, (start + CHUNK) // QP)
        parts = [flat_ref[image * NQ : image * NQ + QP, :] for image in images]
        target = jnp.concatenate([jnp.where(inside, part, 0.0) for part in parts], axis=0)
        joined_t = (target + positions).astype(bf16).T
        grad_query = gq_ref[rows, :]
        grad_key = gk_ref[rows, :]
        grad_value = gv_ref[rows, :]
        add_row(BIAS + 0, total(grad_query.astype(f32)))
        add_row(BIAS + 1, total(grad_value.astype(f32)))
        dw_ref[0] += nn(joined_t, grad_query)
        dw_ref[1] += nn(joined_t, grad_key)
        dw_ref[2] += tn(target.astype(bf16), grad_value)
        grad_joined = nt(grad_query, w_ref[0]) + nt(grad_key, w_ref[1])
        grad_rows_ref[rows, :] += grad_joined + nt(grad_value, w_ref[2])
        grad_place = grad_joined + place_ref[rows, :]
        for image in range(CHUNK // QP):
            drows_ref[POS : POS + QP, :] += grad_place[image * QP : (image + 1) * QP, :]
    for image in range(IMG_MAX):
        part = grad_rows_ref[image * QP : image * QP + NQ, :]
        dtarget_ref[0, image * NQ : (image + 1) * NQ, :] = part

    @pl.when(pack == pl.num_programs(0) - 1)
    def _():
        small = drows_ref[...].T
        dw_ref[SMALL, :, POS:] = small[:, POS:]
        dw_ref[SMALL, :, :POS] = small[:, :POS] + dhead_ref[...]
        half, height, unused = keep_ref.shape
        parts = 2 * half
        share = D // parts
        used = (SMALL + 1) * share
        if height > used:
            block_ref[:, used:, :] = jnp.zeros((parts, height - used, D), f32)

        @pl.loop(0, parts)
        def _(device):
            place = place_of(device, bounds, ordered, parts)
            rows = pl.ds(pl.multiple_of(device * share, share), share)
            for unit in range(SMALL + 1):
                block_ref[place, unit * share : (unit + 1) * share, :] = dw_ref[unit, rows, :]

        keep_ref[...] = block_ref[0:half]
        send_ref[...] = block_ref[half:].astype(bf16)


def whole(shape):
    zeros = (0,) * len(shape)
    return pl.BlockSpec(shape, lambda *unused: zeros)


def by_pack(shape):
    zeros = (0,) * (len(shape) - 1)
    return pl.BlockSpec((1,) + tuple(shape[1:]), lambda pack, *unused: (pack,) + zeros)


LIMIT = 60 * 1024 * 1024


def params(axes):
    return pltpu.CompilerParams(
        dimension_semantics=("arbitrary",) * axes, vmem_limit_bytes=LIMIT
    )


def early_self(bounds, target, memory, memory_pos, mine, other, ordered):
    packs, slots, unused = target.shape
    tokens = memory.shape[1]
    height = mine.shape[1]
    wide = HEADS * QP
    low_rows = jax.ShapeDtypeStruct((packs, ROWS, D), bf16)
    rows = jax.ShapeDtypeStruct((packs, ROWS, D), f32)
    low_tokens = jax.ShapeDtypeStruct((packs, tokens, D), bf16)
    mean = jax.ShapeDtypeStruct((packs, 1, D), f32)
    outs = [rows] + [low_rows] * 4 + [rows, low_rows, low_tokens, low_tokens, mean]
    units = jax.ShapeDtypeStruct((SMALL + 1, D, D), bf16)
    return pl.pallas_call(
        functools.partial(early_self_kernel, ordered),
        grid_spec=pltpu.PrefetchScalarGridSpec(
            num_scalar_prefetch=1,
            grid=(packs,),
            in_specs=[
                by_pack(target.shape),
                by_pack(memory.shape),
                by_pack(memory_pos.shape),
                whole(mine.shape),
                whole(other.shape),
            ],
            out_specs=[by_pack(out.shape) for out in outs] + [whole(units.shape)],
            scratch_shapes=[
                pltpu.VMEM((D, D), f32),
                pltpu.VMEM((slots + 32, D), f32),
                pltpu.VMEM((ROWS, D), f32),
                pltpu.VMEM((2, wide, D), bf16),
                pltpu.VMEM((2 * mine.shape[0], height, D), bf16),
                pltpu.VMEM((SMALL + 1, D, D), f32),
            ],
        ),
        out_shape=outs + [units],
        compiler_params=params(1),
        cost_estimate=pl.CostEstimate(
            flops=packs * 8_000_000_000, bytes_accessed=packs * 9_000_000, transcendentals=0
        ),
        name="early_self",
    )(bounds, target, memory, memory_pos, mine, other)


def early_cross(bounds, rows, query, key, value, mean, weights, slots):
    packs = rows.shape[0]
    tokens = key.shape[1]
    wide = HEADS * QP
    outs = [
        jax.ShapeDtypeStruct((packs, slots, D), f32),
        jax.ShapeDtypeStruct(query.shape, bf16),
        jax.ShapeDtypeStruct((packs, IMG_MAX, 1, wide), f32),
    ]
    arrays = [rows, query, key, value, mean]
    return pl.pallas_call(
        early_cross_kernel,
        grid_spec=pltpu.PrefetchScalarGridSpec(
            num_scalar_prefetch=1,
            grid=(packs,),
            in_specs=[by_pack(array.shape) for array in arrays]
            + [
                pl.BlockSpec((1, D, D), lambda *unused: (7, 0, 0)),
                pl.BlockSpec((1, D, D), lambda *unused: (SMALL, 0, 0)),
            ],
            out_specs=[by_pack(out.shape) for out in outs],
            scratch_shapes=[
                pltpu.VMEM((ROWS, D), f32),
                pltpu.VMEM((wide, D), bf16),
                pltpu.VMEM((tokens, wide), f32),
                pltpu.VMEM((1, wide), f32),
                pltpu.VMEM((1, wide), f32),
                pltpu.VMEM((QP, D), f32),
                pltpu.VMEM((1, D), f32),
            ],
        ),
        out_shape=outs,
        compiler_params=params(1),
        cost_estimate=pl.CostEstimate(
            flops=packs * 8_000_000_000, bytes_accessed=packs * 7_000_000, transcendentals=0
        ),
        name="early_cross",
    )(bounds, *arrays, weights, weights)


def middle(bounds, x, cotangents, mine, other, small, head_bias, ordered):
    packs, slots, unused = x.shape
    half, height, unused = mine.shape
    outs = [
        jax.ShapeDtypeStruct(x.shape, bf16),
        jax.ShapeDtypeStruct(x.shape, f32),
        jax.ShapeDtypeStruct(mine.shape, f32),
        jax.ShapeDtypeStruct(mine.shape, bf16),
        jax.ShapeDtypeStruct((D, POS), f32),
        jax.ShapeDtypeStruct((32, D), f32),
    ]
    return pl.pallas_call(
        functools.partial(middle_kernel, ordered),
        grid_spec=pltpu.PrefetchScalarGridSpec(
            num_scalar_prefetch=1,
            grid=(packs,),
            in_specs=[
                by_pack(x.shape),
                *[by_pack(array.shape) for array in cotangents],
                whole(mine.shape),
                whole(other.shape),
                pl.BlockSpec((1, D, D), lambda *unused: (SMALL, 0, 0)),
                whole(head_bias.shape),
            ],
            out_specs=[by_pack(x.shape), by_pack(x.shape)] + [whole(out.shape) for out in outs[2:]],
            scratch_shapes=[
                pltpu.VMEM((D, D), f32),
                pltpu.VMEM((2 * FF_BLOCKS, 1, D), f32),
                pltpu.VMEM((2, D, D), bf16),
                pltpu.VMEM((slots, D), bf16),
                pltpu.VMEM((slots, D), f32),
                pltpu.VMEM((slots, D), f32),
                pltpu.VMEM((slots, D), bf16),
                pltpu.VMEM((FF_BLOCKS, slots, D), bf16),
                pltpu.VMEM((FF_BLOCKS, slots, D), f32),
                pltpu.VMEM((2 * half, height, D), bf16),
                pltpu.VMEM((2 * half, height, D), f32),
                pltpu.VMEM((2, D, D), f32),
            ],
        ),
        out_shape=outs,
        compiler_params=params(1),
        cost_estimate=pl.CostEstimate(
            flops=packs * 10_000_000_000, bytes_accessed=packs * 9_000_000, transcendentals=0
        ),
        name="middle",
    )(bounds, x, *cotangents, mine, other, small, head_bias)


def late_cross(bounds, grad, memory, memory_pos, weights, saved):
    packs, slots, unused = grad.shape
    tokens = memory.shape[1]
    wide = HEADS * QP
    outs = [
        jax.ShapeDtypeStruct((packs, ROWS, D), bf16),
        jax.ShapeDtypeStruct(memory.shape, f32),
        jax.ShapeDtypeStruct((3, D, D), f32),
        jax.ShapeDtypeStruct((8, D), f32),
    ]
    return pl.pallas_call(
        late_cross_kernel,
        grid_spec=pltpu.PrefetchScalarGridSpec(
            num_scalar_prefetch=1,
            grid=(packs,),
            in_specs=[
                by_pack(grad.shape),
                by_pack(memory.shape),
                by_pack(memory_pos.shape),
                whole(weights.shape),
            ]
            + [by_pack(array.shape) for array in saved],
            out_specs=[by_pack(outs[0].shape), by_pack(outs[1].shape)]
            + [whole(out.shape) for out in outs[2:]],
            scratch_shapes=[
                pltpu.VMEM((slots + 32, D), f32),
                pltpu.VMEM((ROWS, D), f32),
                pltpu.VMEM((ROWS, D), bf16),
                pltpu.VMEM((tokens, D), f32),
                pltpu.VMEM((wide, D), bf16),
                pltpu.VMEM((wide, D), bf16),
                pltpu.VMEM((SIZES[-1], wide), bf16),
                pltpu.VMEM((SIZES[-1], wide), bf16),
                pltpu.VMEM((1, wide), f32),
                pltpu.VMEM((QP, D), f32),
            ],
        ),
        out_shape=outs,
        compiler_params=params(1),
        cost_estimate=pl.CostEstimate(
            flops=packs * 12_000_000_000, bytes_accessed=packs * 9_000_000, transcendentals=0
        ),
        name="late_cross",
    )(bounds, grad, memory, memory_pos, weights, *saved)


def late_self(bounds, grad, grad_query, target, weights, saved, sums, block, ordered):
    packs, slots, unused = target.shape
    wide = HEADS * QP
    half, height, unused = block
    outs = [
        jax.ShapeDtypeStruct(target.shape, f32),
        jax.ShapeDtypeStruct(block, f32),
        jax.ShapeDtypeStruct(block, bf16),
    ]
    return pl.pallas_call(
        functools.partial(late_self_kernel, ordered),
        grid_spec=pltpu.PrefetchScalarGridSpec(
            num_scalar_prefetch=1,
            grid=(packs,),
            in_specs=[
                by_pack(grad.shape),
                by_pack(grad_query.shape),
                by_pack(target.shape),
                whole(weights.shape),
            ]
            + [by_pack(array.shape) for array in saved]
            + [whole(array.shape) for array in sums],
            out_specs=[by_pack(target.shape), whole(block), whole(block)],
            scratch_shapes=[
                pltpu.VMEM((D, D), f32),
                pltpu.VMEM((slots + 32, D), f32),
                pltpu.VMEM((ROWS, D), f32),
                pltpu.VMEM((ROWS, D), f32),
                pltpu.VMEM((ROWS, D), bf16),
                pltpu.VMEM((ROWS, D), bf16),
                pltpu.VMEM((ROWS, D), bf16),
                pltpu.VMEM((ROWS, D), bf16),
                pltpu.VMEM((2, wide, D), bf16),
                pltpu.VMEM((2, wide, D), bf16),
                pltpu.VMEM((2 * QP, wide), bf16),
                pltpu.VMEM((2 * QP, wide), bf16),
                pltpu.VMEM((D, D), f32),
                pltpu.VMEM(weights.shape, f32),
                pltpu.VMEM((2 * half, height, D), f32),
            ],
        ),
        out_shape=outs,
        compiler_params=params(1),
        cost_estimate=pl.CostEstimate(
            flops=packs * 10_000_000_000, bytes_accessed=packs * 7_000_000, transcendentals=0
        ),
        name="late_self",
    )(bounds, grad, grad_query, target, weights, *saved, *sums)


def stack(parts):
    return jnp.concatenate(parts, axis=0)


def fold(keep, received, count):
    for part in received:
        keep = keep + part.astype(f32)
    size = keep.shape[0] // count
    pieces = [keep[index * size : (index + 1) * size] for index in range(count)]
    return pieces[:1] + [piece.astype(bf16) for piece in pieces[1:]]


def run_of_images(segment, me):
    edge = jnp.arange(16, dtype=jnp.int32)
    below = segment[:, None, :] < edge[None, :, None]
    counts = jnp.sum(below.astype(jnp.int32), axis=-1)
    images = jnp.max(jnp.where(segment < IMG_MAX, segment + 1, 0), axis=-1)
    result = jnp.where(edge[None, :] == IMG_MAX + 1, images[:, None], counts)
    return jnp.where(edge[None, :] == ME, me, result)


def taller(rows):
    return jnp.pad(rows, ((0, -rows.shape[0] % 16), (0, 0)))


def pack_early(project, output, classes, box_final, query_pos, gains, biases):
    share = project.shape[1]
    columns = [
        classes,
        box_final,
        gains.T,
        biases.T,
        jnp.zeros((share, POS - BIAS - 13), bf16),
        query_pos.T,
        jnp.zeros((share, D - POS - NQ), bf16),
    ]
    small = jnp.concatenate(columns, axis=1)
    return taller(jnp.concatenate([project.reshape(-1, D), output.reshape(-1, D), small], axis=0))


def pack_middle(box, shrink, expand, expand_bias):
    extra = jnp.pad(expand_bias[None], ((1, EXTRA - 2), (0, D - expand_bias.shape[0])))
    return taller(jnp.concatenate([shrink, expand.T, box[0], box[1], extra], axis=0))


def pack_kernel(
    project,
    output,
    classes,
    final_t,
    gains,
    shifts_t,
    places_t,
    shrink,
    expand_t,
    box,
    row,
    out,
):
    share = project.shape[1]
    small = nn(classes[...], lanes_of(CLS, 0, D)) + tn(final_t[...], lanes_of(4, CLS, D))
    small += tn(gains[...], lanes_of(4, GAIN, D)) + nn(shifts_t[...], lanes_of(13, BIAS, D))
    small += nn(places_t[...], lanes_of(NQ, POS, D))
    first = [project[...].astype(f32).reshape(-1, D), output[...].astype(f32).reshape(-1, D), small]
    first = jnp.concatenate(first, axis=0)
    rest = -first.shape[0] % 16
    count = row.shape[1]
    vector = nn(row[...], lanes_of(count, 0, D))
    index = lax.broadcasted_iota(jnp.int32, (EXTRA, 1), 0)
    extra = jnp.where(index == 1, vector, 0.0)
    blocks = [first, jnp.zeros((rest, D), f32), shrink[...].astype(f32), expand_t[...].astype(f32)]
    blocks += [box[...].astype(f32).reshape(2 * share, D), extra]
    out[...] = jnp.concatenate(blocks, axis=0).astype(bf16)


def pack_both(project, output, classes, final, places, gains, shifts, box, shrink, expand, row):
    share = project.shape[1]
    early_rows = (SMALL + 1) * share
    early_rows += -early_rows % 16
    if share % 8:
        first = pack_early(project, output, classes, final, places, gains, shifts)
        return jnp.concatenate([first, pack_middle(box, shrink, expand, row)]), early_rows
    rows = early_rows + 2 * shrink.shape[0] + 2 * share + EXTRA
    block = pl.pallas_call(
        pack_kernel,
        out_shape=jax.ShapeDtypeStruct((rows, D), bf16),
        name="pack",
    )(
        project,
        output,
        classes,
        final.T,
        gains,
        shifts.T,
        places.T,
        shrink,
        expand.T,
        box,
        row[None],
    )
    return block, early_rows


def block_rows(devices):
    return [FF_BLOCKS * D // devices] * 2 + [D // devices] * 2


def cut(blocks, devices):
    marks = [0]
    for rows in block_rows(devices):
        marks.append(marks[-1] + rows)
    return [blocks[:, low:high] for low, high in zip(marks, marks[1:])], blocks[:, marks[-1] :]


def regroup(blocks, devices, parts):
    pieces, extra = cut(blocks, devices)
    pieces = [piece.reshape(parts, -1, D) for piece in pieces]
    head = jnp.broadcast_to(extra[0:1, 0:1], (parts, 1, D))
    row = extra[:, 1, : FF_BLOCKS * D // devices].reshape(parts, 1, -1)
    row = jnp.pad(row, ((0, 0), (0, EXTRA - 2), (0, D - row.shape[2])))
    result = jnp.concatenate(pieces + [head, row], axis=1)
    return jnp.pad(result, ((0, 0), (0, -result.shape[1] % 16), (0, 0)))


def regroup_units(blocks, devices, parts):
    units = SMALL + 1
    share = D // devices
    result = blocks[:, : units * share].reshape(devices, units, share, D).swapaxes(0, 1)
    result = result.reshape(units, parts, D // parts, D).swapaxes(0, 1).reshape(parts, -1, D)
    return jnp.pad(result, ((0, 0), (0, -result.shape[1] % 16), (0, 0)))


def parts_of(devices):
    return devices if FF_BLOCKS * D // devices % 16 == 0 else FF_BLOCKS


def bit_groups(devices):
    bits = [1 << k for k in range(1, devices.bit_length() - 1)]
    groups = [(1,)]
    while bits:
        groups.append((bits[0], bits[-1]) if len(bits) > 1 else (bits[0],))
        bits = bits[1:-1]
    return groups


def order_of(distance, devices):
    place = 0
    for bits in bit_groups(devices):
        for bit in bits[::-1]:
            place = 2 * place + distance // bit % 2
    return place


def mixes(bits):
    result = [0]
    for bit in bits:
        result += [mix | bit for mix in result]
    return result


def swap(value, bits, devices):
    return lax.ppermute(value, AXES, [(k, k ^ bits) for k in range(devices)])


def trade(held, bits, devices):
    return [swap(held, mix, devices) if mix else held for mix in mixes(bits)]


def deliver(sends, bits, devices):
    return [swap(send, mix, devices) for mix, send in zip(mixes(bits)[1:], sends)]


def counted(blocks, devices, me):
    places = [order_of(device, devices) for device in range(devices)]
    order = jnp.array(places)[jnp.arange(devices) ^ me]
    return jnp.take(blocks, order, axis=0)


def stepped(blocks, devices, me):
    distances = [0] * devices
    for device in range(devices):
        distances[order_of(device, devices)] = device
    return jnp.take(blocks, jnp.array(distances) ^ me, axis=0)


def unpack_middle(block, devices):
    pieces, extra = cut(block[None], devices)
    shrink, expand, box_one, box_two = [piece[0] for piece in pieces]
    row = extra[0, 1, 0 : shrink.shape[0]]
    return shrink, expand.T, jnp.stack([box_one, box_two]), row, extra[0, 0, 0 : CLS + 4]


def finish_kernel(count, keep, *refs):
    total_block = keep[0]
    for ref in refs[:count]:
        total_block += ref[0].astype(f32)
    project, output, classes, final_t, places_t, gains, shifts_t = refs[count:]
    share = project.shape[1]
    project[...] = total_block[: 6 * share].reshape(6, share, D)
    output[...] = total_block[6 * share : 8 * share].reshape(2, share, D)
    small = total_block[8 * share : 9 * share]
    classes[...] = small[:, 0:CLS]
    places_t[...] = small[:, POS : POS + NQ]
    shifts_t[...] = small[:, BIAS : BIAS + 13]
    turned = small[:, 0:POS].T
    final_t[...] = turned[CLS : CLS + 4]
    gains[...] = turned[GAIN : GAIN + 4]


def finish_early(keep, received, devices):
    share = D // devices
    if share % 8:
        return unpack_early(fold(keep, received, 1)[0][0], devices)
    shapes = [(6, share, D), (2, share, D), (share, CLS), (4, share), (share, NQ), (4, share)]
    shapes.append((share, 13))
    project, output, classes, final_t, places_t, gains, shifts_t = pl.pallas_call(
        functools.partial(finish_kernel, len(received)),
        out_shape=[jax.ShapeDtypeStruct(shape, f32) for shape in shapes],
        name="finish",
    )(keep, *received)
    return project, output, classes, final_t.T, places_t.T, gains, shifts_t.T


def unpack_early(block, devices):
    units = SMALL + 1
    share = D // devices
    block = block[: units * share].reshape(units, share, D)
    small = block[SMALL]
    return (
        block[0:6],
        block[6:8],
        small[:, 0:CLS],
        small[:, CLS : CLS + 4],
        small[:, POS : POS + NQ].T,
        small[:, GAIN : GAIN + 4].T,
        small[:, BIAS : BIAS + 13].T,
    )


def per_device(
    target,
    memory,
    memory_pos,
    segment,
    project_weight,
    output_weight,
    expand_weight,
    shrink_weight,
    box_weight,
    class_weight,
    box_final,
    query_pos,
    norm_gains,
    biases,
    expand_bias,
    head_bias,
    output_cotangent,
    logit_cotangent,
    box_cotangent,
):
    devices = lax.axis_size(AXES)
    me = lax.axis_index(AXES)
    groups = bit_groups(devices)
    parts = parts_of(devices)
    ordered = parts == devices
    slots = target.shape[1]

    both, height = pack_both(
        project_weight,
        output_weight,
        class_weight,
        box_final,
        query_pos,
        norm_gains,
        biases,
        box_weight,
        shrink_weight,
        expand_weight,
        expand_bias,
    )
    both = both[None]
    both_parts = trade(both, groups[-1], devices)
    both_parts, logit_cotangent, box_cotangent = lax.optimization_barrier(
        (both_parts, logit_cotangent, box_cotangent)
    )
    early_held = stack([part[:, :height] for part in both_parts])
    middle_held = stack([part[:, height:] for part in both_parts])
    for bits in groups[-2:1:-1]:
        early_held = stack(trade(early_held, bits, devices))
    early_parts = trade(early_held, groups[1], devices)
    bounds = run_of_images(segment, me)
    head_row = jnp.pad(head_bias.astype(f32), (0, POS - CLS - 4))
    head_row = jnp.broadcast_to(head_row[None], (8, POS))
    rest = jnp.zeros(logit_cotangent.shape[:2] + (POS - CLS - 4,), bf16)
    head_cotangent = jnp.concatenate([logit_cotangent, box_cotangent, rest], axis=-1)
    early_parts, bounds, head_row, head_cotangent, middle_held = lax.optimization_barrier(
        (early_parts, bounds, head_row, head_cotangent, middle_held)
    )
    early_mine = stack(early_parts)
    early_other = swap(early_mine, 1, devices)
    if not ordered:
        blocks = counted(jnp.concatenate([early_mine, early_other]), devices, me)
        blocks = regroup_units(blocks, devices, parts)
        early_mine, early_other = blocks[: parts // 2], blocks[parts // 2 :]
    middle_parts = trade(middle_held, groups[-2], devices)
    rows, *saved = early_self(
        bounds, target, memory, memory_pos, early_mine, early_other, ordered
    )
    query, key, value, mean, weights = saved[5:]
    middle_parts, query = lax.optimization_barrier((middle_parts, query))
    for bits in groups[-3:0:-1]:
        middle_parts = trade(stack(middle_parts), bits, devices)
    middle_mine = stack(middle_parts)
    middle_mine, query = lax.optimization_barrier((middle_mine, query))
    middle_other = swap(middle_mine, 1, devices)
    after, context, logs = early_cross(bounds, rows, query, key, value, mean, weights, slots)
    if not ordered:
        blocks = counted(jnp.concatenate([middle_mine, middle_other]), devices, me)
        blocks = regroup(blocks, devices, parts)
        middle_mine, middle_other = blocks[: parts // 2], blocks[parts // 2 :]
    layer, grad, keep, send, dhead, drow = middle(
        bounds,
        after,
        [output_cotangent, head_cotangent],
        middle_mine,
        middle_other,
        weights,
        head_row,
        ordered,
    )

    def real_blocks(keep, send, change):
        if ordered:
            return keep, send
        blocks = jnp.concatenate([keep, send.astype(f32)])
        blocks = stepped(change(blocks, parts, devices), devices, me)
        return blocks[: devices // 2], blocks[devices // 2 :].astype(bf16)

    def counts(index):
        return 1 << len(groups[index]) if index < len(groups) else 1

    keep, send = real_blocks(keep, send, regroup)
    grad, keep, send = lax.optimization_barrier((grad, keep, send))
    received = deliver([send], groups[0], devices)
    grad_query, dmemory, dcross, dcross_rows = late_cross(
        bounds, grad, memory, memory_pos, weights, [query, key, value, context, logs]
    )
    grad_query, received = lax.optimization_barrier((grad_query, received))
    keep, *sends = fold(keep, received, counts(1))
    grad_query, keep, sends = lax.optimization_barrier((grad_query, keep, sends))
    received = deliver(sends, groups[1], devices)
    sums = [dcross, dcross_rows, dhead, drow]
    block = early_mine.shape
    dtarget, early_keep, early_send = late_self(
        bounds, grad, grad_query, target, weights, saved[:5], sums, block, ordered
    )
    early_keep, early_send, received = lax.optimization_barrier(
        (early_keep, early_send, received)
    )
    early_keep, early_send = real_blocks(early_keep, early_send, regroup_units)
    early_received = deliver([early_send], groups[0], devices)
    for index in range(2, len(groups)):
        keep, *sends = fold(keep, received, counts(index))
        received = deliver(sends, groups[index], devices)
    early_keep, *early_sends = fold(early_keep, early_received, counts(1))
    early_received = deliver(early_sends, groups[1], devices)
    early_received, received = lax.optimization_barrier((early_received, received))
    for index in range(2, len(groups)):
        early_keep, *early_sends = fold(early_keep, early_received, counts(index))
        early_received = deliver(early_sends, groups[index], devices)
    middle_sum = fold(keep, received, 1)[0]
    middle_grads = unpack_middle(middle_sum[0], devices)
    early_received, middle_grads = lax.optimization_barrier((early_received, middle_grads))
    shrink, expand, box, expand_row, head = middle_grads
    project, output, classes, final, places, gains, shifts = finish_early(
        early_keep, early_received, devices
    )
    return (
        layer,
        dtarget,
        dmemory,
        project,
        output,
        expand,
        shrink,
        box,
        classes,
        final,
        places,
        gains,
        shifts,
        expand_row,
        head,
    )


def solution(mesh):
    both = ("dp", "fsdp")
    by_rows = P(both, None, None)
    return jax.shard_map(
        per_device,
        mesh=mesh,
        in_specs=(
            by_rows,
            by_rows,
            by_rows,
            P(both, None),
            P(None, both, None),
            P(None, both, None),
            P(None, both),
            P(both, None),
            P(None, both, None),
            P(both, None),
            P(both, None),
            P(None, both),
            P(None, both),
            P(None, both),
            P(both),
            P(),
            by_rows,
            by_rows,
            by_rows,
        ),
        out_specs=(
            by_rows,
            by_rows,
            by_rows,
            P(None, both, None),
            P(None, both, None),
            P(None, both),
            P(both, None),
            P(None, both, None),
            P(both, None),
            P(both, None),
            P(None, both),
            P(None, both),
            P(None, both),
            P(both),
            P(),
        ),
        check_vma=False,
    )
```

profile of v0, /device:TPU:0, one launch (start us, length us, event | category | flops | bytes accessed | tf_op | source)
XLA Modules:
  0.0 241.2 jit_solution(12641240155637258528)
XLA Ops:
  0.7 1.7 pack.1
  2.4 5.0 %collective-permute-start.2 = (bf16[1,240,256]{2,1,0:T(8,128)(2,1)}, bf16[1,240,256]{2,1,0:T(8,128)(2,1)S(1)}, u32[]{:S(2)}, u32[]{:S(2)}) collective-permute-start(bf16[1,240,256]{2,1,0:T(8,128)(2,1)} %bitcast.19), channel_id=1, source_target_pairs={{0,12},{1,13},{2,14},{3,15},{4,8},{5,9},{6,10},{7,11},{8,4},{9,5},... | collective-permute-start | bytes 368648 | tf_op jit(solution)/shard_map/ppermute | solution.py:1312
  7.5 0.6 collective-permute-start
  8.0 0.8 fusion.4
  8.9 0.9 convert_reduce_fusion
  9.7 0.6 select_select_fusion.bounds
  10.4 0.1 pad.21.clone
  10.5 0.7 pad_convert_fusion
  11.1 0.8 collective-permute-done.2
  11.9 6.1 %collective-permute-done.1 = bf16[1,240,256]{2,1,0:T(8,128)(2,1)S(1)} collective-permute-done((bf16[1,240,256]{2,1,0:T(8,128)(2,1)}, bf16[1,240,256]{2,1,0:T(8,128)(2,1)S(1)}, u32[]{:S(2)}, u32[]{:S(2)}) %collective-permute-start.1) | collective-permute-done | bytes 122912 | tf_op jit(solution)/shard_map/ppermute | solution.py:1312
  18.0 0.8 slice.105
  18.9 2.5 %collective-permute-start.5 = (bf16[4,80,256]{2,1,0:T(8,128)(2,1)S(1)}, bf16[4,80,256]{2,1,0:T(8,128)(2,1)S(1)}, u32[]{:S(2)}, u32[]{:S(2)}) collective-permute-start(bf16[4,80,256]{2,1,0:T(8,128)(2,1)S(1)} %pad_maximum_fusion.2), channel_id=1, source_target_pairs={{0,18},{1,19},{2,16},{3,17},{4,22},{5,23},{6,20},{7,21},{8,26},{9,... | collective-permute-start | bytes 491528 | tf_op jit(solution)/shard_map/ppermute | solution.py:1312
  21.4 0.5 collective-permute-start.4
  21.9 0.5 collective-permute-start.3
  22.4 1.6 copy.36
  24.1 0.4 copy.37
  24.5 1.2 maximum_maximum_fusion.head_cot_ref
  25.8 0.5 collective-permute-done.5
  26.3 2.3 collective-permute-done.4
  28.6 0.1 collective-permute-done.3
  28.7 0.6 broadcast_in_dim.59.head_bias_ref
  29.3 0.1 collective-permute-start.6
  29.4 1.8 collective-permute-start.9
  31.2 1.3 collective-permute-start.8
  32.5 0.5 collective-permute-start.7
  33.0 0.8 copy-done.10
  33.8 24.8 %early_self.1 = (f32[2,1536,256]{2,1,0:T(8,128)}, bf16[2,1536,256]{2,1,0:T(8,128)(2,1)}, bf16[2,1536,256]{2,1,0:T(8,128)(2,1)}, bf16[2,1536,256]{2,1,0:T(8,128)(...) custom-call(s32[2,16]{1,0:T(2,128)} %select_select_fusion.bounds, ...), custom_call_target="tpu_custom_call" | custom-call | flops 16000000000 | bytes 18000000 | tf_op jit(solution)/shard_map/early_self/pallas_call | solution.py:935
  58.7 0.2 pad_maximum_fusion.mine_ref
  58.9 0.1 collective-permute-start.10
  59.0 25.3 %early_cross.1 = (f32[2,1200,256]{2,1,0:T(8,128)}, bf16[2,1536,256]{2,1,0:T(8,128)(2,1)}, f32[2,12,1,1024]{3,2,1,0:T(1,128)}) custom-call(s32[2,16]{1,0:T(2,128)} %select_select_fusion.bounds, f32[2,1536,256]{2,1,0:T(8,128)} %get-tuple-element.110.rows_in_ref, bf16[2,1536,256]{2,1,0:T(8,128)(2,1)} %get-tuple-element.118.cq_ref, ...), custom_call_target="tpu_custom_call" | custom-call | flops 16000000000 | bytes 14000000 | tf_op jit(solution)/shard_map/early_cross/pallas_call | solution.py:976
  84.3 1.0 copy-done.9
  85.4 50.7 %middle.1 = (bf16[2,1200,256]{2,1,0:T(8,128)(2,1)}, f32[2,1200,256]{2,1,0:T(8,128)}, f32[16,160,256]{2,1,0:T(8,128)}, bf16[16,160,256]{2,1,0:T(8,128)(2,1)}, f32[256,128]{1,0:T(8,128)}, /*index=5*/f32[32,256]{1,0:T(8,128)}) custom-call(s32[2,16]{1,0:T(2,128)} %select_select_fusion.bounds, f32[2,1200,256]{2,1,0:T(8,128)} %get-tuple-element.123.x_ref, ...), custom_call_target="tpu_custom_call" | custom-call | flops 20000000000 | bytes 18000000 | tf_op jit(solution)/shard_map/middle/pallas_call | solution.py:1017
  136.1 0.1 collective-permute-start.11
  136.1 35.9 %late_cross.1 = (bf16[2,1536,256]{2,1,0:T(8,128)(2,1)}, f32[2,2048,256]{2,1,0:T(8,128)}, f32[3,256,256]{2,1,0:T(8,128)}, f32[8,256]{1,0:T(8,128)}) custom-call(s32[2,16]{1,0:T(2,128)} %select_select_fusion.bounds, f32[2,1200,256]{2,1,0:T(8,128)} %get-tuple-element.131.grad_ref, bf16[2,2048,256]{2,1,0:T(8,128)(2,1)} %memory_ref.3, ...), custom_call_target="tpu_custom_call" | custom-call | flops 24000000000 | bytes 18000000 | tf_op jit(solution)/shard_map/late_cross/pallas_call | solution.py:1065
  172.1 0.4 fusion.9
  172.5 0.1 fusion.10
  172.6 0.9 collective-permute-start.12
  173.5 2.7 %collective-permute-start.14 = (bf16[4,160,256]{2,1,0:T(8,128)(2,1)S(1)}, bf16[4,160,256]{2,1,0:T(8,128)(2,1)S(1)}, u32[]{:S(2)}, u32[]{:S(2)}) collective-permute-start(bf16[4,160,256]{2,1,0:T(8,128)(2,1)S(1)} %get-tuple-element.155), channel_id=1, source_target_pairs={{0,18},{1,19},{2,16},{3,17},{4,22},{5,23},{6,20},{7,21},{8,26},{9,... | collective-permute-start | bytes 983048 | tf_op jit(solution)/shard_map/ppermute | solution.py:1312
  176.2 32.2 %late_self.1 = (f32[2,1200,256]{2,1,0:T(8,128)}, f32[16,80,256]{2,1,0:T(8,128)}, bf16[16,80,256]{2,1,0:T(8,128)(2,1)}) custom-call(s32[2,16]{1,0:T(2,128)} %select_select_fusion.bounds, f32[2,1200,256]{2,1,0:T(8,128)} %get-tuple-element.131.grad_ref, bf16[2,1536,256]{2,1,0:T(8,128)(2,1)} %get-tuple-element.139.gcq_ref, bf16[2,1200,256]{2,1,0:T(8,128)(2,1)} %target_ref.3, ...), custom_call_target="tpu_custom_call" | custom-call | flops 20000000000 | bytes 14000000 | tf_op jit(solution)/shard_map/late_self/pallas_call | solution.py:1110
  208.5 3.6 %collective-permute-start.15 = (bf16[16,80,256]{2,1,0:T(8,128)(2,1)}, bf16[16,80,256]{2,1,0:T(8,128)(2,1)S(1)}, u32[]{:S(2)}, u32[]{:S(2)}) collective-permute-start(bf16[16,80,256]{2,1,0:T(8,128)(2,1)} %get-tuple-element.157), channel_id=1, source_target_pairs={{0,1},{1,0},{2,3},{3,2},{4,5},{5,4},{6,7},{7,6},{8,9},{9,8},{10,11... | collective-permute-start | bytes 1966088 | tf_op jit(solution)/shard_map/ppermute | solution.py:1312
  212.0 0.2 fusion.7
  212.2 7.5 %collective-permute-start.21 = (bf16[1,160,256]{2,1,0:T(8,128)(2,1)S(1)}, bf16[1,160,256]{2,1,0:T(8,128)(2,1)S(1)}, u32[]{:S(2)}, u32[]{:S(2)}) collective-permute-start(bf16[1,160,256]{2,1,0:T(8,128)(2,1)S(1)} %get-tuple-element.197), channel_id=1, source_target_pairs={{0,12},{1,13},{2,14},{3,15},{4,8},{5,9},{6,10},{7,11},{8,4},{9,5},... | collective-permute-start | bytes 245768 | tf_op jit(solution)/shard_map/ppermute | solution.py:1312
  219.8 0.2 fusion.8
  220.0 0.1 collective-permute-start.18
  220.1 1.5 collective-permute-start.17
  221.6 2.0 collective-permute-start.16
  223.5 2.6 %collective-permute-start.19 = (bf16[1,160,256]{2,1,0:T(8,128)(2,1)S(1)}, bf16[1,160,256]{2,1,0:T(8,128)(2,1)S(1)}, u32[]{:S(2)}, u32[]{:S(2)}) collective-permute-start(bf16[1,160,256]{2,1,0:T(8,128)(2,1)S(1)} %get-tuple-element.199), channel_id=1, source_target_pairs={{0,4},{1,5},{2,6},{3,7},{4,0},{5,1},{6,2},{7,3},{8,12},{9,13},{10,... | collective-permute-start | bytes 245768 | tf_op jit(solution)/shard_map/ppermute | solution.py:1312
  226.1 3.1 %collective-permute-done.20 = bf16[1,160,256]{2,1,0:T(8,128)(2,1)S(1)} collective-permute-done((bf16[1,160,256]{2,1,0:T(8,128)(2,1)S(1)}, bf16[1,160,256]{2,1,0:T(8,128)(2,1)S(1)}, u32[]{:S(2)}, u32[]{:S(2)}) %collective-permute-start.20) | collective-permute-done | bytes 81952 | tf_op jit(solution)/shard_map/ppermute | solution.py:1312
  229.3 0.4 collective-permute-done.19
  229.7 0.3 collective-permute-done.17
  230.0 0.5 slice_bitcast_fusion.3
  230.5 0.5 slice_bitcast_fusion.2
  231.0 0.7 slice_bitcast_fusion
  231.7 0.1 fusion.5
  231.8 2.1 collective-permute-start.24
  233.9 0.1 collective-permute-start.23
  233.9 2.3 collective-permute-start.22
  236.2 0.6 pad_maximum_fusion.3
  236.8 0.6 slice.146.keep
  237.5 0.3 collective-permute-done.24.refs_2_
  237.8 1.2 collective-permute-done.23.refs_1_
  239.0 0.6 copy-done.6
  239.6 0.0 copy-done.7
  239.6 1.6 finish.1
  (57 shorter events, 0.4 us)
Async XLA Ops:
  0.7 23.4 %copy-start.8 = (bf16[2,1200,4]{1,2,0:T(4,128)(2,1)S(1)}, bf16[2,1200,4]{1,2,0:T(4,128)(2,1)}, u32[]{:S(2)}) copy-start(bf16[2,1200,4]{1,2,0:T(4,128)(2,1)} %param.37) | copy-start | bytes 57604
  2.4 9.5 %collective-permute-start.2 = (bf16[1,240,256]{2,1,0:T(8,128)(2,1)}, bf16[1,240,256]{2,1,0:T(8,128)(2,1)S(1)}, u32[]{:S(2)}, u32[]{:S(2)}) collective-permute-start(bf16[1,240,256]{2,1,0:T(8,128)(2,1)} %bitcast.19), channel_id=1, source_target_pairs={{0,12},{1,13},{2,14},{3,15},{4,8},{5,9},{6,10},{7,11},{8,4},{9,5},... | collective-permute-start | bytes 368648 | tf_op jit(solution)/shard_map/ppermute | solution.py:1312
  7.4 10.6 %collective-permute-start.1 = (bf16[1,240,256]{2,1,0:T(8,128)(2,1)}, bf16[1,240,256]{2,1,0:T(8,128)(2,1)S(1)}, u32[]{:S(2)}, u32[]{:S(2)}) collective-permute-start(bf16[1,240,256]{2,1,0:T(8,128)(2,1)} %bitcast.20), channel_id=1, source_target_pairs={{0,8},{1,9},{2,10},{3,11},{4,12},{5,13},{6,14},{7,15},{8,0},{9,1},... | collective-permute-start | bytes 368648 | tf_op jit(solution)/shard_map/ppermute | solution.py:1312
  7.5 10.6 %collective-permute-start = (bf16[1,240,256]{2,1,0:T(8,128)(2,1)}, bf16[1,240,256]{2,1,0:T(8,128)(2,1)S(1)}, u32[]{:S(2)}, u32[]{:S(2)}) collective-permute-start(bf16[1,240,256]{2,1,0:T(8,128)(2,1)} %bitcast.21), channel_id=1, source_target_pairs={{0,4},{1,5},{2,6},{3,7},{4,0},{5,1},{6,2},{7,3},{8,12},{9,13},{10,... | collective-permute-start | bytes 368648 | tf_op jit(solution)/shard_map/ppermute | solution.py:1312
  18.9 7.5 %collective-permute-start.5 = (bf16[4,80,256]{2,1,0:T(8,128)(2,1)S(1)}, bf16[4,80,256]{2,1,0:T(8,128)(2,1)S(1)}, u32[]{:S(2)}, u32[]{:S(2)}) collective-permute-start(bf16[4,80,256]{2,1,0:T(8,128)(2,1)S(1)} %pad_maximum_fusion.2), channel_id=1, source_target_pairs={{0,18},{1,19},{2,16},{3,17},{4,22},{5,23},{6,20},{7,21},{8,26},{9,... | collective-permute-start | bytes 491528 | tf_op jit(solution)/shard_map/ppermute | solution.py:1312
  21.4 7.2 %collective-permute-start.4 = (bf16[4,80,256]{2,1,0:T(8,128)(2,1)S(1)}, bf16[4,80,256]{2,1,0:T(8,128)(2,1)S(1)}, u32[]{:S(2)}, u32[]{:S(2)}) collective-permute-start(bf16[4,80,256]{2,1,0:T(8,128)(2,1)S(1)} %pad_maximum_fusion.2), channel_id=1, source_target_pairs={{0,16},{1,17},{2,18},{3,19},{4,20},{5,21},{6,22},{7,23},{8,24},{9,... | collective-permute-start | bytes 491528 | tf_op jit(solution)/shard_map/ppermute | solution.py:1312
  21.9 6.8 %collective-permute-start.3 = (bf16[4,80,256]{2,1,0:T(8,128)(2,1)S(1)}, bf16[4,80,256]{2,1,0:T(8,128)(2,1)S(1)}, u32[]{:S(2)}, u32[]{:S(2)}) collective-permute-start(bf16[4,80,256]{2,1,0:T(8,128)(2,1)S(1)} %pad_maximum_fusion.2), channel_id=1, source_target_pairs={{0,2},{1,3},{2,0},{3,1},{4,6},{5,7},{6,4},{7,5},{8,10},{9,11},{10,... | collective-permute-start | bytes 491528 | tf_op jit(solution)/shard_map/ppermute | solution.py:1312
  24.1 1.6 copy-start.3
  29.3 3.7 %copy-start.4 = (bf16[16,80,256]{2,1,0:T(8,128)(2,1)}, bf16[16,80,256]{2,1,0:T(8,128)(2,1)S(1)}, u32[]{:S(2)}) copy-start(bf16[16,80,256]{2,1,0:T(8,128)(2,1)S(1)} %constant_dynamic-update-slice_fusion.mine_ref) | copy-start | bytes 1966084
  29.3 3.6 %collective-permute-start.6 = (bf16[16,80,256]{2,1,0:T(8,128)(2,1)S(1)}, bf16[16,80,256]{2,1,0:T(8,128)(2,1)S(1)}, u32[]{:S(2)}, u32[]{:S(2)}) collective-permute-start(bf16[16,80,256]{2,1,0:T(8,128)(2,1)S(1)} %constant_dynamic-update-slice_fusion.mine_ref), channel_id=1, source_target_pairs={{0,1},{1,0},{2,3},{3,2},{4,5},{5,4},{6,7},{7,6},{8,9},{9,8},{10,11... | collective-permute-start | bytes 1966088 | tf_op jit(solution)/shard_map/ppermute | solution.py:1312
  29.4 29.3 %collective-permute-start.9 = (bf16[4,160,256]{2,1,0:T(8,128)(2,1)S(1)}, bf16[4,160,256]{2,1,0:T(8,128)(2,1)S(1)}, u32[]{:S(2)}, u32[]{:S(2)}) collective-permute-start(bf16[4,160,256]{2,1,0:T(8,128)(2,1)S(1)} %pad_maximum_fusion.1), channel_id=1, source_target_pairs={{0,18},{1,19},{2,16},{3,17},{4,22},{5,23},{6,20},{7,21},{8,26},{9,... | collective-permute-start | bytes 983048 | tf_op jit(solution)/shard_map/ppermute | solution.py:1312
  31.2 27.5 %collective-permute-start.8 = (bf16[4,160,256]{2,1,0:T(8,128)(2,1)S(1)}, bf16[4,160,256]{2,1,0:T(8,128)(2,1)S(1)}, u32[]{:S(2)}, u32[]{:S(2)}) collective-permute-start(bf16[4,160,256]{2,1,0:T(8,128)(2,1)S(1)} %pad_maximum_fusion.1), channel_id=1, source_target_pairs={{0,16},{1,17},{2,18},{3,19},{4,20},{5,21},{6,22},{7,23},{8,24},{9,... | collective-permute-start | bytes 983048 | tf_op jit(solution)/shard_map/ppermute | solution.py:1312
  32.5 26.2 %collective-permute-start.7 = (bf16[4,160,256]{2,1,0:T(8,128)(2,1)S(1)}, bf16[4,160,256]{2,1,0:T(8,128)(2,1)S(1)}, u32[]{:S(2)}, u32[]{:S(2)}) collective-permute-start(bf16[4,160,256]{2,1,0:T(8,128)(2,1)S(1)} %pad_maximum_fusion.1), channel_id=1, source_target_pairs={{0,2},{1,3},{2,0},{3,1},{4,6},{5,7},{6,4},{7,5},{8,10},{9,11},{10,... | collective-permute-start | bytes 983048 | tf_op jit(solution)/shard_map/ppermute | solution.py:1312
  33.0 0.8 copy-start.10
  58.9 25.4 %copy-start.1 = (bf16[16,160,256]{2,1,0:T(8,128)(2,1)}, bf16[16,160,256]{2,1,0:T(8,128)(2,1)S(1)}, u32[]{:S(2)}) copy-start(bf16[16,160,256]{2,1,0:T(8,128)(2,1)S(1)} %pad_maximum_fusion.mine_ref) | copy-start | bytes 3932164
  58.9 25.4 %collective-permute-start.10 = (bf16[16,160,256]{2,1,0:T(8,128)(2,1)S(1)}, bf16[16,160,256]{2,1,0:T(8,128)(2,1)S(1)}, u32[]{:S(2)}, u32[]{:S(2)}) collective-permute-start(bf16[16,160,256]{2,1,0:T(8,128)(2,1)S(1)} %pad_maximum_fusion.mine_ref), channel_id=1, source_target_pairs={{0,1},{1,0},{2,3},{3,2},{4,5},{5,4},{6,7},{7,6},{8,9},{9,8},{10,11... | collective-permute-start | bytes 3932168 | tf_op jit(solution)/shard_map/ppermute | solution.py:1312
  84.3 1.1 copy-start.9
  136.1 36.0 %collective-permute-start.11 = (bf16[16,160,256]{2,1,0:T(8,128)(2,1)}, bf16[16,160,256]{2,1,0:T(8,128)(2,1)S(1)}, u32[]{:S(2)}, u32[]{:S(2)}) collective-permute-start(bf16[16,160,256]{2,1,0:T(8,128)(2,1)} %get-tuple-element.135), channel_id=1, source_target_pairs={{0,1},{1,0},{2,3},{3,2},{4,5},{5,4},{6,7},{7,6},{8,9},{9,8},{10,11... | collective-permute-start | bytes 3932168 | tf_op jit(solution)/shard_map/ppermute | solution.py:1312
  136.1 35.9 %copy-start = (f32[16,160,256]{2,1,0:T(8,128)S(1)}, f32[16,160,256]{2,1,0:T(8,128)}, u32[]{:S(2)}) copy-start(f32[16,160,256]{2,1,0:T(8,128)} %get-tuple-element.137) | copy-start | bytes 7864324
  172.6 35.8 %collective-permute-start.12 = (bf16[4,160,256]{2,1,0:T(8,128)(2,1)S(1)}, bf16[4,160,256]{2,1,0:T(8,128)(2,1)S(1)}, u32[]{:S(2)}, u32[]{:S(2)}) collective-permute-start(bf16[4,160,256]{2,1,0:T(8,128)(2,1)S(1)} %get-tuple-element.153), channel_id=1, source_target_pairs={{0,2},{1,3},{2,0},{3,1},{4,6},{5,7},{6,4},{7,5},{8,10},{9,11},{10,... | collective-permute-start | bytes 983048 | tf_op jit(solution)/shard_map/ppermute | solution.py:1312
  173.5 34.9 %collective-permute-start.13 = (bf16[4,160,256]{2,1,0:T(8,128)(2,1)S(1)}, bf16[4,160,256]{2,1,0:T(8,128)(2,1)S(1)}, u32[]{:S(2)}, u32[]{:S(2)}) collective-permute-start(bf16[4,160,256]{2,1,0:T(8,128)(2,1)S(1)} %get-tuple-element.154), channel_id=1, source_target_pairs={{0,16},{1,17},{2,18},{3,19},{4,20},{5,21},{6,22},{7,23},{8,24},{9,... | collective-permute-start | bytes 983048 | tf_op jit(solution)/shard_map/ppermute | solution.py:1312
  173.5 34.9 %collective-permute-start.14 = (bf16[4,160,256]{2,1,0:T(8,128)(2,1)S(1)}, bf16[4,160,256]{2,1,0:T(8,128)(2,1)S(1)}, u32[]{:S(2)}, u32[]{:S(2)}) collective-permute-start(bf16[4,160,256]{2,1,0:T(8,128)(2,1)S(1)} %get-tuple-element.155), channel_id=1, source_target_pairs={{0,18},{1,19},{2,16},{3,17},{4,22},{5,23},{6,20},{7,21},{8,26},{9,... | collective-permute-start | bytes 983048 | tf_op jit(solution)/shard_map/ppermute | solution.py:1312
  208.5 11.3 %copy-start.2 = (f32[16,80,256]{2,1,0:T(8,128)S(1)}, f32[16,80,256]{2,1,0:T(8,128)}, u32[]{:S(2)}) copy-start(f32[16,80,256]{2,1,0:T(8,128)} %get-tuple-element.156) | copy-start | bytes 3932164
  208.5 11.3 %collective-permute-start.15 = (bf16[16,80,256]{2,1,0:T(8,128)(2,1)}, bf16[16,80,256]{2,1,0:T(8,128)(2,1)S(1)}, u32[]{:S(2)}, u32[]{:S(2)}) collective-permute-start(bf16[16,80,256]{2,1,0:T(8,128)(2,1)} %get-tuple-element.157), channel_id=1, source_target_pairs={{0,1},{1,0},{2,3},{3,2},{4,5},{5,4},{6,7},{7,6},{8,9},{9,8},{10,11... | collective-permute-start | bytes 1966088 | tf_op jit(solution)/shard_map/ppermute | solution.py:1312
  212.2 11.3 %collective-permute-start.21 = (bf16[1,160,256]{2,1,0:T(8,128)(2,1)S(1)}, bf16[1,160,256]{2,1,0:T(8,128)(2,1)S(1)}, u32[]{:S(2)}, u32[]{:S(2)}) collective-permute-start(bf16[1,160,256]{2,1,0:T(8,128)(2,1)S(1)} %get-tuple-element.197), channel_id=1, source_target_pairs={{0,12},{1,13},{2,14},{3,15},{4,8},{5,9},{6,10},{7,11},{8,4},{9,5},... | collective-permute-start | bytes 245768 | tf_op jit(solution)/shard_map/ppermute | solution.py:1312
  220.0 9.7 %collective-permute-start.18 = (bf16[4,80,256]{2,1,0:T(8,128)(2,1)S(1)}, bf16[4,80,256]{2,1,0:T(8,128)(2,1)S(1)}, u32[]{:S(2)}, u32[]{:S(2)}) collective-permute-start(bf16[4,80,256]{2,1,0:T(8,128)(2,1)S(1)} %get-tuple-element.194), channel_id=1, source_target_pairs={{0,18},{1,19},{2,16},{3,17},{4,22},{5,23},{6,20},{7,21},{8,26},{9,... | collective-permute-start | bytes 491528 | tf_op jit(solution)/shard_map/ppermute | solution.py:1312
  220.1 9.9 %collective-permute-start.17 = (bf16[4,80,256]{2,1,0:T(8,128)(2,1)S(1)}, bf16[4,80,256]{2,1,0:T(8,128)(2,1)S(1)}, u32[]{:S(2)}, u32[]{:S(2)}) collective-permute-start(bf16[4,80,256]{2,1,0:T(8,128)(2,1)S(1)} %get-tuple-element.195), channel_id=1, source_target_pairs={{0,16},{1,17},{2,18},{3,19},{4,20},{5,21},{6,22},{7,23},{8,24},{9,... | collective-permute-start | bytes 491528 | tf_op jit(solution)/shard_map/ppermute | solution.py:1312
  221.6 8.4 %collective-permute-start.16 = (bf16[4,80,256]{2,1,0:T(8,128)(2,1)S(1)}, bf16[4,80,256]{2,1,0:T(8,128)(2,1)S(1)}, u32[]{:S(2)}, u32[]{:S(2)}) collective-permute-start(bf16[4,80,256]{2,1,0:T(8,128)(2,1)S(1)} %get-tuple-element.196), channel_id=1, source_target_pairs={{0,2},{1,3},{2,0},{3,1},{4,6},{5,7},{6,4},{7,5},{8,10},{9,11},{10,... | collective-permute-start | bytes 491528 | tf_op jit(solution)/shard_map/ppermute | solution.py:1312
  223.5 5.7 %collective-permute-start.20 = (bf16[1,160,256]{2,1,0:T(8,128)(2,1)S(1)}, bf16[1,160,256]{2,1,0:T(8,128)(2,1)S(1)}, u32[]{:S(2)}, u32[]{:S(2)}) collective-permute-start(bf16[1,160,256]{2,1,0:T(8,128)(2,1)S(1)} %get-tuple-element.198), channel_id=1, source_target_pairs={{0,8},{1,9},{2,10},{3,11},{4,12},{5,13},{6,14},{7,15},{8,0},{9,1},... | collective-permute-start | bytes 245768 | tf_op jit(solution)/shard_map/ppermute | solution.py:1312
  223.5 6.1 %collective-permute-start.19 = (bf16[1,160,256]{2,1,0:T(8,128)(2,1)S(1)}, bf16[1,160,256]{2,1,0:T(8,128)(2,1)S(1)}, u32[]{:S(2)}, u32[]{:S(2)}) collective-permute-start(bf16[1,160,256]{2,1,0:T(8,128)(2,1)S(1)} %get-tuple-element.199), channel_id=1, source_target_pairs={{0,4},{1,5},{2,6},{3,7},{4,0},{5,1},{6,2},{7,3},{8,12},{9,13},{10,... | collective-permute-start | bytes 245768 | tf_op jit(solution)/shard_map/ppermute | solution.py:1312
  231.8 6.0 %collective-permute-start.24 = (bf16[1,80,256]{2,1,0:T(8,128)(2,1)S(1)}, bf16[1,80,256]{2,1,0:T(8,128)(2,1)S(1)}, u32[]{:S(2)}, u32[]{:S(2)}) collective-permute-start(bf16[1,80,256]{2,1,0:T(8,128)(2,1)S(1)} %get-tuple-element.204), channel_id=1, source_target_pairs={{0,12},{1,13},{2,14},{3,15},{4,8},{5,9},{6,10},{7,11},{8,4},{9,5},... | collective-permute-start | bytes 122888 | tf_op jit(solution)/shard_map/ppermute | solution.py:1312
  233.9 5.1 %collective-permute-start.23 = (bf16[1,80,256]{2,1,0:T(8,128)(2,1)S(1)}, bf16[1,80,256]{2,1,0:T(8,128)(2,1)S(1)}, u32[]{:S(2)}, u32[]{:S(2)}) collective-permute-start(bf16[1,80,256]{2,1,0:T(8,128)(2,1)S(1)} %get-tuple-element.205), channel_id=1, source_target_pairs={{0,8},{1,9},{2,10},{3,11},{4,12},{5,13},{6,14},{7,15},{8,0},{9,1},... | collective-permute-start | bytes 122888 | tf_op jit(solution)/shard_map/ppermute | solution.py:1312
  233.9 5.0 %collective-permute-start.22 = (bf16[1,80,256]{2,1,0:T(8,128)(2,1)S(1)}, bf16[1,80,256]{2,1,0:T(8,128)(2,1)S(1)}, u32[]{:S(2)}, u32[]{:S(2)}) collective-permute-start(bf16[1,80,256]{2,1,0:T(8,128)(2,1)S(1)} %get-tuple-element.206), channel_id=1, source_target_pairs={{0,4},{1,5},{2,6},{3,7},{4,0},{5,1},{6,2},{7,3},{8,12},{9,13},{10,... | collective-permute-start | bytes 122888 | tf_op jit(solution)/shard_map/ppermute | solution.py:1312
  237.8 1.2 copy-start.5
  238.9 0.6 copy-start.6
  238.9 0.6 copy-start.7
where the time goes:
time: 241 us
  Pallas kernels  172 us (71%)
  starting transfers between devices  38.2 us (16%)
  waiting for transfers between devices  15.1 us (6%)
  local copies, waits for them, and re-layouts  8.61 us (4%)
  other arithmetic  5.94 us (2%)
    pallas_call x1, Pallas kernels, middle(): pl.pallas_call(functools.partial(middle_kernel, ordered), grid_spec=pltpu...  50.7 us
    ppermute x25, starting transfers between devices, swap(): return lax.ppermute(value, AXES, [(k, k ^ bits) for k in range(devices)])  38.2 us
    pallas_call x1, Pallas kernels, late_cross(): pl.pallas_call(late_cross_kernel, grid_spec=pltpu.PrefetchScalarGridSpec(...  35.9 us
    pallas_call x1, Pallas kernels, late_self(): pl.pallas_call(functools.partial(late_self_kernel, ordered), grid_spec=pl...  32.2 us
    pallas_call x1, Pallas kernels, early_cross(): pl.pallas_call(early_cross_kernel, grid_spec=pltpu.PrefetchScalarGridSpec...  25.3 us
    pallas_call x1, Pallas kernels, early_self(): pl.pallas_call(functools.partial(early_self_kernel, ordered), grid_spec=p...  24.8 us
    ppermute x25, waiting for transfers between devices, swap(): return lax.ppermute(value, AXES, [(k, k ^ bits) for k in range(devices)])  15.1 us
  transfers between devices with their start and end apart: 25, of which 10 were waited for; matrix products, arithmetic and copies ran while one was open for 3% of the time, Pallas kernels for 49%

commit v1 on v0

--- a/solution.py
+++ b/solution.py
@@ -15,6 +15,7 @@
 HEAD_DIM = 32
 QP = 128
 ROWS = IMG_MAX * QP
+TURNS = 3
 PAIRS = HEADS // 2
 BLOCK = 256
 SIZES = (128, 192, 256, 384, 512)
@@ -183,6 +184,7 @@
     ck_ref,
     cv_ref,
     mean_ref,
+    log_ref,
     w_ref,
     small_ref,
     flat_ref,
@@ -246,16 +248,17 @@
         ks_ref[0, rows, :] = nn(joined, w_ref[1]).astype(bf16)
         vs_ref[0, rows, :] = (nn(target.astype(bf16), w_ref[2]) + bias(1)).astype(bf16)
 
-    @pl.loop(0, IMG_MAX // 2)
+    @pl.loop(0, IMG_MAX // TURNS)
     def _(step):
-        for turn in range(2):
-            rows = pl.ds(pl.multiple_of((2 * step + turn) * QP, QP), QP)
+        for turn in range(TURNS):
+            rows = pl.ds(pl.multiple_of((TURNS * step + turn) * QP, QP), QP)
             spread = spread_ref.at[turn]
             spread_heads(qs_ref[0, rows, :], spread)
-            context, unused = attend_block(
+            context, logs = attend_block(
                 ks_ref[0, rows, :], vs_ref[0, rows, :], spread, inside, True
             )
             cs_ref[0, rows, :] = context.astype(bf16)
+            log_ref[0, TURNS * step + turn] = logs
 
     @chunk_loop(ROWS, CHUNK)
     def _(start, rows):
@@ -575,14 +578,8 @@
     lows = []
     for pair in range(PAIRS):
         lanes = slice(2 * QP * pair, 2 * QP * (pair + 1))
-        if logs is None:
-            kept = jnp.where(valid, scores[pair], masked)
-            top = jnp.max(kept, axis=0, keepdims=True)
-            raised = jnp.exp2((kept - top) * (scale * log2e))
-            attend = raised * (1.0 / total(raised))
-        else:
-            attend = jnp.exp2(scores[pair] * (scale * log2e) - logs[:, lanes])
-            attend = jnp.where(valid, attend, 0.0)
+        attend = jnp.exp2(scores[pair] * (scale * log2e) - logs[:, lanes])
+        attend = jnp.where(valid, attend, 0.0)
         row_dot = total(attend * grads[pair])
         low = (attend * (grads[pair] - row_dot)).astype(bf16)
         attend_ref[:, lanes] = attend.astype(bf16)
@@ -757,6 +754,7 @@
     vs_ref,
     cs_ref,
     inner_ref,
+    log_ref,
     dcross_ref,
     dcross_rows_ref,
     dhead_ref,
@@ -832,10 +830,10 @@
         dw_ref[6] += tn(cs_ref[0, rows, :], branch)
         context_ref[rows, :] = nt(branch, w_ref[6]).astype(bf16)
 
-    @pl.loop(0, IMG_MAX // 2)
+    @pl.loop(0, IMG_MAX // TURNS)
     def _(step):
-        for turn in range(2):
-            rows = pl.ds(pl.multiple_of((2 * step + turn) * QP, QP), QP)
+        for turn in range(TURNS):
+            rows = pl.ds(pl.multiple_of((TURNS * step + turn) * QP, QP), QP)
             spread = spread_ref.at[turn]
             spread_grad = spread_grad_ref.at[turn]
             attend_low = attend_ref.at[turn * QP : (turn + 1) * QP]
@@ -848,7 +846,7 @@
                 spread,
                 spread_grad,
                 inside,
-                None,
+                log_ref[0, TURNS * step + turn],
                 attend_low,
                 score_low,
             )
@@ -930,7 +928,8 @@
     rows = jax.ShapeDtypeStruct((packs, ROWS, D), f32)
     low_tokens = jax.ShapeDtypeStruct((packs, tokens, D), bf16)
     mean = jax.ShapeDtypeStruct((packs, 1, D), f32)
-    outs = [rows] + [low_rows] * 4 + [rows, low_rows, low_tokens, low_tokens, mean]
+    logs = jax.ShapeDtypeStruct((packs, IMG_MAX, 1, wide), f32)
+    outs = [rows] + [low_rows] * 4 + [rows, low_rows, low_tokens, low_tokens, mean, logs]
     units = jax.ShapeDtypeStruct((SMALL + 1, D, D), bf16)
     return pl.pallas_call(
         functools.partial(early_self_kernel, ordered),
@@ -949,7 +948,7 @@
                 pltpu.VMEM((D, D), f32),
                 pltpu.VMEM((slots + 32, D), f32),
                 pltpu.VMEM((ROWS, D), f32),
-                pltpu.VMEM((2, wide, D), bf16),
+                pltpu.VMEM((TURNS, wide, D), bf16),
                 pltpu.VMEM((2 * mine.shape[0], height, D), bf16),
                 pltpu.VMEM((SMALL + 1, D, D), f32),
             ],
@@ -1130,10 +1129,10 @@
                 pltpu.VMEM((ROWS, D), bf16),
                 pltpu.VMEM((ROWS, D), bf16),
                 pltpu.VMEM((ROWS, D), bf16),
-                pltpu.VMEM((2, wide, D), bf16),
-                pltpu.VMEM((2, wide, D), bf16),
-                pltpu.VMEM((2 * QP, wide), bf16),
-                pltpu.VMEM((2 * QP, wide), bf16),
+                pltpu.VMEM((TURNS, wide, D), bf16),
+                pltpu.VMEM((TURNS, wide, D), bf16),
+                pltpu.VMEM((TURNS * QP, wide), bf16),
+                pltpu.VMEM((TURNS * QP, wide), bf16),
                 pltpu.VMEM((D, D), f32),
                 pltpu.VMEM(weights.shape, f32),
                 pltpu.VMEM((2 * half, height, D), f32),
@@ -1456,7 +1455,7 @@
     rows, *saved = early_self(
         bounds, target, memory, memory_pos, early_mine, early_other, ordered
     )
-    query, key, value, mean, weights = saved[5:]
+    query, key, value, mean, self_logs, weights = saved[5:]
     middle_parts, query = lax.optimization_barrier((middle_parts, query))
     for bits in groups[-3:0:-1]:
         middle_parts = trade(stack(middle_parts), bits, devices)
@@ -1501,8 +1500,9 @@
     received = deliver(sends, groups[1], devices)
     sums = [dcross, dcross_rows, dhead, drow]
     block = early_mine.shape
+    late_saved = saved[:5] + [self_logs]
     dtarget, early_keep, early_send = late_self(
-        bounds, grad, grad_query, target, weights, saved[:5], sums, block, ordered
+        bounds, grad, grad_query, target, weights, late_saved, sums, block, ordered
     )
     early_keep, early_send, received = lax.optimization_barrier(
         (early_keep, early_send, received)

time: 241 us -> 233 us (0.967)
  starting transfers between devices: 38.2 us -> 32 us
  Pallas kernels: 172 us -> 169 us
    ppermute x25, starting transfers between devices: 38.2 us -> 32 us  [swap(): return lax.ppermute(value, AXES, [(k, k ^ bits) for k in range(devices)])]
  transfers between devices with their start and end apart: 25 -> 25, of which waited for: 10 -> 12; matrix products, arithmetic and copies ran while one was open for 3% -> 3% of each run, Pallas kernels for 49% -> 49%
where the time goes in v1:
time: 233 us
  Pallas kernels  169 us (73%)
  starting transfers between devices  32 us (14%)
  waiting for transfers between devices  17.3 us (7%)
  local copies, waits for them, and re-layouts  8.61 us (4%)
  other arithmetic  5.94 us (3%)
    pallas_call x1, Pallas kernels, middle(): pl.pallas_call(functools.partial(middle_kernel, ordered), grid_spec=pltpu...  50.7 us
    pallas_call x1, Pallas kernels, late_cross(): pl.pallas_call(late_cross_kernel, grid_spec=pltpu.PrefetchScalarGridSpec(...  36 us
    ppermute x25, starting transfers between devices, swap(): return lax.ppermute(value, AXES, [(k, k ^ bits) for k in range(devices)])  32 us
    pallas_call x1, Pallas kernels, late_self(): pl.pallas_call(functools.partial(late_self_kernel, ordered), grid_spec=pl...  30.5 us
    pallas_call x1, Pallas kernels, early_cross(): pl.pallas_call(early_cross_kernel, grid_spec=pltpu.PrefetchScalarGridSpec...  24.3 us
    pallas_call x1, Pallas kernels, early_self(): pl.pallas_call(functools.partial(early_self_kernel, ordered), grid_spec=p...  23.7 us
    ppermute x25, waiting for transfers between devices, swap(): return lax.ppermute(value, AXES, [(k, k ^ bits) for k in range(devices)])  17.3 us
  transfers between devices with their start and end apart: 25, of which 12 were waited for; matrix products, arithmetic and copies ran while one was open for 3% of the time, Pallas kernels for 49%

profile of v1, /device:TPU:0, one launch (start us, length us, event | category | flops | bytes accessed | tf_op | source)
XLA Modules:
  0.0 233.4 jit_solution(14862677450971325842)
XLA Ops:
  0.7 1.7 pack.1
  2.4 5.0 %collective-permute-start.2 = (bf16[1,240,256]{2,1,0:T(8,128)(2,1)}, bf16[1,240,256]{2,1,0:T(8,128)(2,1)S(1)}, u32[]{:S(2)}, u32[]{:S(2)}) collective-permute-start(bf16[1,240,256]{2,1,0:T(8,128)(2,1)} %bitcast.19), channel_id=1, source_target_pairs={{0,12},{1,13},{2,14},{3,15},{4,8},{5,9},{6,10},{7,11},{8,4},{9,5},... | collective-permute-start | bytes 368648 | tf_op jit(solution)/shard_map/ppermute | solution.py:1311
  7.5 0.6 collective-permute-start
  8.0 0.8 fusion.4
  8.9 0.9 convert_reduce_fusion
  9.7 0.6 select_select_fusion.bounds
  10.4 0.1 pad.21.clone
  10.5 0.7 pad_convert_fusion
  11.1 0.8 collective-permute-done.2
  11.9 6.1 %collective-permute-done.1 = bf16[1,240,256]{2,1,0:T(8,128)(2,1)S(1)} collective-permute-done((bf16[1,240,256]{2,1,0:T(8,128)(2,1)}, bf16[1,240,256]{2,1,0:T(8,128)(2,1)S(1)}, u32[]{:S(2)}, u32[]{:S(2)}) %collective-permute-start.1) | collective-permute-done | bytes 122912 | tf_op jit(solution)/shard_map/ppermute | solution.py:1311
  18.0 0.8 slice.105
  18.9 2.5 %collective-permute-start.5 = (bf16[4,80,256]{2,1,0:T(8,128)(2,1)S(1)}, bf16[4,80,256]{2,1,0:T(8,128)(2,1)S(1)}, u32[]{:S(2)}, u32[]{:S(2)}) collective-permute-start(bf16[4,80,256]{2,1,0:T(8,128)(2,1)S(1)} %pad_maximum_fusion.2), channel_id=1, source_target_pairs={{0,18},{1,19},{2,16},{3,17},{4,22},{5,23},{6,20},{7,21},{8,26},{9,... | collective-permute-start | bytes 491528 | tf_op jit(solution)/shard_map/ppermute | solution.py:1311
  21.4 0.5 collective-permute-start.4
  21.9 0.5 collective-permute-start.3
  22.4 1.6 copy.36
  24.1 0.4 copy.37
  24.5 1.2 maximum_maximum_fusion.head_cot_ref
  25.8 0.5 collective-permute-done.5
  26.3 2.3 collective-permute-done.4
  28.7 0.6 broadcast_in_dim.59.head_bias_ref
  29.3 0.1 collective-permute-start.6
  29.4 1.8 collective-permute-start.9
  31.2 1.3 collective-permute-start.8
  32.5 0.5 collective-permute-start.7
  33.0 0.8 copy-done.10
  33.8 23.7 %early_self.1 = (f32[2,1536,256]{2,1,0:T(8,128)}, bf16[2,1536,256]{2,1,0:T(8,128)(2,1)}, bf16[2,1536,256]{2,1,0:T(8,128)(2,1)}, bf16[2,1536,256]{2,1,0:T(8,128)(...) custom-call(s32[2,16]{1,0:T(2,128)} %select_select_fusion.bounds, ...), custom_call_target="tpu_custom_call" | custom-call | flops 16000000000 | bytes 18000000 | tf_op jit(solution)/shard_map/early_self/pallas_call | solution.py:934
  57.5 0.2 pad_maximum_fusion.mine_ref
  57.7 0.1 collective-permute-start.10
  57.8 24.3 %early_cross.1 = (f32[2,1200,256]{2,1,0:T(8,128)}, bf16[2,1536,256]{2,1,0:T(8,128)(2,1)}, f32[2,12,1,1024]{3,2,1,0:T(1,128)}) custom-call(s32[2,16]{1,0:T(2,128)} %select_select_fusion.bounds, f32[2,1536,256]{2,1,0:T(8,128)} %get-tuple-element.111.rows_in_ref, bf16[2,1536,256]{2,1,0:T(8,128)(2,1)} %get-tuple-element.119.cq_ref, ...), custom_call_target="tpu_custom_call" | custom-call | flops 16000000000 | bytes 14000000 | tf_op jit(solution)/shard_map/early_cross/pallas_call | solution.py:975
  82.2 1.0 copy-done.9
  83.2 50.7 %middle.1 = (bf16[2,1200,256]{2,1,0:T(8,128)(2,1)}, f32[2,1200,256]{2,1,0:T(8,128)}, f32[16,160,256]{2,1,0:T(8,128)}, bf16[16,160,256]{2,1,0:T(8,128)(2,1)}, f32[256,128]{1,0:T(8,128)}, /*index=5*/f32[32,256]{1,0:T(8,128)}) custom-call(s32[2,16]{1,0:T(2,128)} %select_select_fusion.bounds, f32[2,1200,256]{2,1,0:T(8,128)} %get-tuple-element.124.x_ref, ...), custom_call_target="tpu_custom_call" | custom-call | flops 20000000000 | bytes 18000000 | tf_op jit(solution)/shard_map/middle/pallas_call | solution.py:1016
  133.9 2.2 collective-permute-start.11
  136.1 36.0 %late_cross.1 = (bf16[2,1536,256]{2,1,0:T(8,128)(2,1)}, f32[2,2048,256]{2,1,0:T(8,128)}, f32[3,256,256]{2,1,0:T(8,128)}, f32[8,256]{1,0:T(8,128)}) custom-call(s32[2,16]{1,0:T(2,128)} %select_select_fusion.bounds, f32[2,1200,256]{2,1,0:T(8,128)} %get-tuple-element.132.grad_ref, bf16[2,2048,256]{2,1,0:T(8,128)(2,1)} %memory_ref.3, ...), custom_call_target="tpu_custom_call" | custom-call | flops 24000000000 | bytes 18000000 | tf_op jit(solution)/shard_map/late_cross/pallas_call | solution.py:1064
  172.2 0.4 fusion.9
  172.7 0.1 collective-permute-start.12
  172.8 0.5 collective-permute-start.13
  173.3 3.0 %collective-permute-start.14 = (bf16[4,160,256]{2,1,0:T(8,128)(2,1)S(1)}, bf16[4,160,256]{2,1,0:T(8,128)(2,1)S(1)}, u32[]{:S(2)}, u32[]{:S(2)}) collective-permute-start(bf16[4,160,256]{2,1,0:T(8,128)(2,1)S(1)} %get-tuple-element.157), channel_id=1, source_target_pairs={{0,18},{1,19},{2,16},{3,17},{4,22},{5,23},{6,20},{7,21},{8,26},{9,... | collective-permute-start | bytes 983048 | tf_op jit(solution)/shard_map/ppermute | solution.py:1311
  176.3 30.5 %late_self.1 = (f32[2,1200,256]{2,1,0:T(8,128)}, f32[16,80,256]{2,1,0:T(8,128)}, bf16[16,80,256]{2,1,0:T(8,128)(2,1)}) custom-call(s32[2,16]{1,0:T(2,128)} %select_select_fusion.bounds, f32[2,1200,256]{2,1,0:T(8,128)} %get-tuple-element.132.grad_ref, bf16[2,1536,256]{2,1,0:T(8,128)(2,1)} %get-tuple-element.140.gcq_ref, bf16[2,1200,256]{2,1,0:T(8,128)(2,1)} %target_ref.3, ...), custom_call_target="tpu_custom_call" | custom-call | flops 20000000000 | bytes 14000000 | tf_op jit(solution)/shard_map/late_self/pallas_call | solution.py:1109
  206.8 3.4 %collective-permute-start.15 = (bf16[16,80,256]{2,1,0:T(8,128)(2,1)}, bf16[16,80,256]{2,1,0:T(8,128)(2,1)S(1)}, u32[]{:S(2)}, u32[]{:S(2)}) collective-permute-start(bf16[16,80,256]{2,1,0:T(8,128)(2,1)} %get-tuple-element.159), channel_id=1, source_target_pairs={{0,1},{1,0},{2,3},{3,2},{4,5},{5,4},{6,7},{7,6},{8,9},{9,8},{10,11... | collective-permute-start | bytes 1966088 | tf_op jit(solution)/shard_map/ppermute | solution.py:1311
  210.1 0.2 fusion.7
  210.3 0.1 collective-permute-start.21
  210.4 1.7 collective-permute-done.15
  212.1 0.2 fusion.8
  212.3 0.4 collective-permute-start.18
  212.7 1.5 collective-permute-start.17
  214.2 1.7 collective-permute-start.16
  215.9 0.8 collective-permute-done.21
  216.7 1.9 collective-permute-start.19
  218.6 3.0 %collective-permute-done.20 = bf16[1,160,256]{2,1,0:T(8,128)(2,1)S(1)} collective-permute-done((bf16[1,160,256]{2,1,0:T(8,128)(2,1)S(1)}, bf16[1,160,256]{2,1,0:T(8,128)(2,1)S(1)}, u32[]{:S(2)}, u32[]{:S(2)}) %collective-permute-start.20) | collective-permute-done | bytes 81952 | tf_op jit(solution)/shard_map/ppermute | solution.py:1311
  221.6 0.4 collective-permute-done.19
  222.1 0.4 collective-permute-done.17
  222.5 0.5 slice_bitcast_fusion.3
  223.0 0.5 slice_bitcast_fusion.2
  223.5 0.7 slice_bitcast_fusion
  224.2 0.1 fusion.5
  224.3 1.6 collective-permute-start.24
  225.9 0.5 collective-permute-start.23
  226.4 2.3 collective-permute-start.22
  228.7 0.6 pad_maximum_fusion.3
  229.3 0.6 slice.146.keep
  230.0 0.3 collective-permute-done.24.refs_2_
  230.3 0.9 collective-permute-done.23.refs_1_
  231.2 0.6 copy-done.6
  231.8 1.6 finish.1
  (57 shorter events, 0.5 us)
Async XLA Ops:
  0.7 23.4 %copy-start.8 = (bf16[2,1200,4]{1,2,0:T(4,128)(2,1)S(1)}, bf16[2,1200,4]{1,2,0:T(4,128)(2,1)}, u32[]{:S(2)}) copy-start(bf16[2,1200,4]{1,2,0:T(4,128)(2,1)} %param.37) | copy-start | bytes 57604
  2.4 9.5 %collective-permute-start.2 = (bf16[1,240,256]{2,1,0:T(8,128)(2,1)}, bf16[1,240,256]{2,1,0:T(8,128)(2,1)S(1)}, u32[]{:S(2)}, u32[]{:S(2)}) collective-permute-start(bf16[1,240,256]{2,1,0:T(8,128)(2,1)} %bitcast.19), channel_id=1, source_target_pairs={{0,12},{1,13},{2,14},{3,15},{4,8},{5,9},{6,10},{7,11},{8,4},{9,5},... | collective-permute-start | bytes 368648 | tf_op jit(solution)/shard_map/ppermute | solution.py:1311
  7.4 10.6 %collective-permute-start.1 = (bf16[1,240,256]{2,1,0:T(8,128)(2,1)}, bf16[1,240,256]{2,1,0:T(8,128)(2,1)S(1)}, u32[]{:S(2)}, u32[]{:S(2)}) collective-permute-start(bf16[1,240,256]{2,1,0:T(8,128)(2,1)} %bitcast.20), channel_id=1, source_target_pairs={{0,8},{1,9},{2,10},{3,11},{4,12},{5,13},{6,14},{7,15},{8,0},{9,1},... | collective-permute-start | bytes 368648 | tf_op jit(solution)/shard_map/ppermute | solution.py:1311
  7.5 10.6 %collective-permute-start = (bf16[1,240,256]{2,1,0:T(8,128)(2,1)}, bf16[1,240,256]{2,1,0:T(8,128)(2,1)S(1)}, u32[]{:S(2)}, u32[]{:S(2)}) collective-permute-start(bf16[1,240,256]{2,1,0:T(8,128)(2,1)} %bitcast.21), channel_id=1, source_target_pairs={{0,4},{1,5},{2,6},{3,7},{4,0},{5,1},{6,2},{7,3},{8,12},{9,13},{10,... | collective-permute-start | bytes 368648 | tf_op jit(solution)/shard_map/ppermute | solution.py:1311
  18.9 7.5 %collective-permute-start.5 = (bf16[4,80,256]{2,1,0:T(8,128)(2,1)S(1)}, bf16[4,80,256]{2,1,0:T(8,128)(2,1)S(1)}, u32[]{:S(2)}, u32[]{:S(2)}) collective-permute-start(bf16[4,80,256]{2,1,0:T(8,128)(2,1)S(1)} %pad_maximum_fusion.2), channel_id=1, source_target_pairs={{0,18},{1,19},{2,16},{3,17},{4,22},{5,23},{6,20},{7,21},{8,26},{9,... | collective-permute-start | bytes 491528 | tf_op jit(solution)/shard_map/ppermute | solution.py:1311
  21.4 7.2 %collective-permute-start.4 = (bf16[4,80,256]{2,1,0:T(8,128)(2,1)S(1)}, bf16[4,80,256]{2,1,0:T(8,128)(2,1)S(1)}, u32[]{:S(2)}, u32[]{:S(2)}) collective-permute-start(bf16[4,80,256]{2,1,0:T(8,128)(2,1)S(1)} %pad_maximum_fusion.2), channel_id=1, source_target_pairs={{0,16},{1,17},{2,18},{3,19},{4,20},{5,21},{6,22},{7,23},{8,24},{9,... | collective-permute-start | bytes 491528 | tf_op jit(solution)/shard_map/ppermute | solution.py:1311
  21.9 6.8 %collective-permute-start.3 = (bf16[4,80,256]{2,1,0:T(8,128)(2,1)S(1)}, bf16[4,80,256]{2,1,0:T(8,128)(2,1)S(1)}, u32[]{:S(2)}, u32[]{:S(2)}) collective-permute-start(bf16[4,80,256]{2,1,0:T(8,128)(2,1)S(1)} %pad_maximum_fusion.2), channel_id=1, source_target_pairs={{0,2},{1,3},{2,0},{3,1},{4,6},{5,7},{6,4},{7,5},{8,10},{9,11},{10,... | collective-permute-start | bytes 491528 | tf_op jit(solution)/shard_map/ppermute | solution.py:1311
  24.1 1.6 copy-start.3
  29.3 3.7 %copy-start.4 = (bf16[16,80,256]{2,1,0:T(8,128)(2,1)}, bf16[16,80,256]{2,1,0:T(8,128)(2,1)S(1)}, u32[]{:S(2)}) copy-start(bf16[16,80,256]{2,1,0:T(8,128)(2,1)S(1)} %constant_dynamic-update-slice_fusion.mine_ref) | copy-start | bytes 1966084
  29.3 3.6 %collective-permute-start.6 = (bf16[16,80,256]{2,1,0:T(8,128)(2,1)S(1)}, bf16[16,80,256]{2,1,0:T(8,128)(2,1)S(1)}, u32[]{:S(2)}, u32[]{:S(2)}) collective-permute-start(bf16[16,80,256]{2,1,0:T(8,128)(2,1)S(1)} %constant_dynamic-update-slice_fusion.mine_ref), channel_id=1, source_target_pairs={{0,1},{1,0},{2,3},{3,2},{4,5},{5,4},{6,7},{7,6},{8,9},{9,8},{10,11... | collective-permute-start | bytes 1966088 | tf_op jit(solution)/shard_map/ppermute | solution.py:1311
  29.4 28.1 %collective-permute-start.9 = (bf16[4,160,256]{2,1,0:T(8,128)(2,1)S(1)}, bf16[4,160,256]{2,1,0:T(8,128)(2,1)S(1)}, u32[]{:S(2)}, u32[]{:S(2)}) collective-permute-start(bf16[4,160,256]{2,1,0:T(8,128)(2,1)S(1)} %pad_maximum_fusion.1), channel_id=1, source_target_pairs={{0,18},{1,19},{2,16},{3,17},{4,22},{5,23},{6,20},{7,21},{8,26},{9,... | collective-permute-start | bytes 983048 | tf_op jit(solution)/shard_map/ppermute | solution.py:1311
  31.2 26.3 %collective-permute-start.8 = (bf16[4,160,256]{2,1,0:T(8,128)(2,1)S(1)}, bf16[4,160,256]{2,1,0:T(8,128)(2,1)S(1)}, u32[]{:S(2)}, u32[]{:S(2)}) collective-permute-start(bf16[4,160,256]{2,1,0:T(8,128)(2,1)S(1)} %pad_maximum_fusion.1), channel_id=1, source_target_pairs={{0,16},{1,17},{2,18},{3,19},{4,20},{5,21},{6,22},{7,23},{8,24},{9,... | collective-permute-start | bytes 983048 | tf_op jit(solution)/shard_map/ppermute | solution.py:1311
  32.5 25.0 %collective-permute-start.7 = (bf16[4,160,256]{2,1,0:T(8,128)(2,1)S(1)}, bf16[4,160,256]{2,1,0:T(8,128)(2,1)S(1)}, u32[]{:S(2)}, u32[]{:S(2)}) collective-permute-start(bf16[4,160,256]{2,1,0:T(8,128)(2,1)S(1)} %pad_maximum_fusion.1), channel_id=1, source_target_pairs={{0,2},{1,3},{2,0},{3,1},{4,6},{5,7},{6,4},{7,5},{8,10},{9,11},{10,... | collective-permute-start | bytes 983048 | tf_op jit(solution)/shard_map/ppermute | solution.py:1311
  33.0 0.8 copy-start.10
  57.7 24.4 %copy-start.1 = (bf16[16,160,256]{2,1,0:T(8,128)(2,1)}, bf16[16,160,256]{2,1,0:T(8,128)(2,1)S(1)}, u32[]{:S(2)}) copy-start(bf16[16,160,256]{2,1,0:T(8,128)(2,1)S(1)} %pad_maximum_fusion.mine_ref) | copy-start | bytes 3932164
  57.7 24.4 %collective-permute-start.10 = (bf16[16,160,256]{2,1,0:T(8,128)(2,1)S(1)}, bf16[16,160,256]{2,1,0:T(8,128)(2,1)S(1)}, u32[]{:S(2)}, u32[]{:S(2)}) collective-permute-start(bf16[16,160,256]{2,1,0:T(8,128)(2,1)S(1)} %pad_maximum_fusion.mine_ref), channel_id=1, source_target_pairs={{0,1},{1,0},{2,3},{3,2},{4,5},{5,4},{6,7},{7,6},{8,9},{9,8},{10,11... | collective-permute-start | bytes 3932168 | tf_op jit(solution)/shard_map/ppermute | solution.py:1311
  82.2 1.1 copy-start.9
  133.9 38.2 %collective-permute-start.11 = (bf16[16,160,256]{2,1,0:T(8,128)(2,1)}, bf16[16,160,256]{2,1,0:T(8,128)(2,1)S(1)}, u32[]{:S(2)}, u32[]{:S(2)}) collective-permute-start(bf16[16,160,256]{2,1,0:T(8,128)(2,1)} %get-tuple-element.136), channel_id=1, source_target_pairs={{0,1},{1,0},{2,3},{3,2},{4,5},{5,4},{6,7},{7,6},{8,9},{9,8},{10,11... | collective-permute-start | bytes 3932168 | tf_op jit(solution)/shard_map/ppermute | solution.py:1311
  136.1 36.0 %copy-start = (f32[16,160,256]{2,1,0:T(8,128)S(1)}, f32[16,160,256]{2,1,0:T(8,128)}, u32[]{:S(2)}) copy-start(f32[16,160,256]{2,1,0:T(8,128)} %get-tuple-element.138) | copy-start | bytes 7864324
  172.7 34.0 %collective-permute-start.12 = (bf16[4,160,256]{2,1,0:T(8,128)(2,1)S(1)}, bf16[4,160,256]{2,1,0:T(8,128)(2,1)S(1)}, u32[]{:S(2)}, u32[]{:S(2)}) collective-permute-start(bf16[4,160,256]{2,1,0:T(8,128)(2,1)S(1)} %get-tuple-element.155), channel_id=1, source_target_pairs={{0,2},{1,3},{2,0},{3,1},{4,6},{5,7},{6,4},{7,5},{8,10},{9,11},{10,... | collective-permute-start | bytes 983048 | tf_op jit(solution)/shard_map/ppermute | solution.py:1311
  172.8 34.0 %collective-permute-start.13 = (bf16[4,160,256]{2,1,0:T(8,128)(2,1)S(1)}, bf16[4,160,256]{2,1,0:T(8,128)(2,1)S(1)}, u32[]{:S(2)}, u32[]{:S(2)}) collective-permute-start(bf16[4,160,256]{2,1,0:T(8,128)(2,1)S(1)} %get-tuple-element.156), channel_id=1, source_target_pairs={{0,16},{1,17},{2,18},{3,19},{4,20},{5,21},{6,22},{7,23},{8,24},{9,... | collective-permute-start | bytes 983048 | tf_op jit(solution)/shard_map/ppermute | solution.py:1311
  173.3 33.5 %collective-permute-start.14 = (bf16[4,160,256]{2,1,0:T(8,128)(2,1)S(1)}, bf16[4,160,256]{2,1,0:T(8,128)(2,1)S(1)}, u32[]{:S(2)}, u32[]{:S(2)}) collective-permute-start(bf16[4,160,256]{2,1,0:T(8,128)(2,1)S(1)} %get-tuple-element.157), channel_id=1, source_target_pairs={{0,18},{1,19},{2,16},{3,17},{4,22},{5,23},{6,20},{7,21},{8,26},{9,... | collective-permute-start | bytes 983048 | tf_op jit(solution)/shard_map/ppermute | solution.py:1311
  206.8 5.3 %copy-start.2 = (f32[16,80,256]{2,1,0:T(8,128)S(1)}, f32[16,80,256]{2,1,0:T(8,128)}, u32[]{:S(2)}) copy-start(f32[16,80,256]{2,1,0:T(8,128)} %get-tuple-element.158) | copy-start | bytes 3932164
  206.8 5.3 %collective-permute-start.15 = (bf16[16,80,256]{2,1,0:T(8,128)(2,1)}, bf16[16,80,256]{2,1,0:T(8,128)(2,1)S(1)}, u32[]{:S(2)}, u32[]{:S(2)}) collective-permute-start(bf16[16,80,256]{2,1,0:T(8,128)(2,1)} %get-tuple-element.159), channel_id=1, source_target_pairs={{0,1},{1,0},{2,3},{3,2},{4,5},{5,4},{6,7},{7,6},{8,9},{9,8},{10,11... | collective-permute-start | bytes 1966088 | tf_op jit(solution)/shard_map/ppermute | solution.py:1311
  210.3 6.3 %collective-permute-start.21 = (bf16[1,160,256]{2,1,0:T(8,128)(2,1)S(1)}, bf16[1,160,256]{2,1,0:T(8,128)(2,1)S(1)}, u32[]{:S(2)}, u32[]{:S(2)}) collective-permute-start(bf16[1,160,256]{2,1,0:T(8,128)(2,1)S(1)} %get-tuple-element.199), channel_id=1, source_target_pairs={{0,12},{1,13},{2,14},{3,15},{4,8},{5,9},{6,10},{7,11},{8,4},{9,5},... | collective-permute-start | bytes 245768 | tf_op jit(solution)/shard_map/ppermute | solution.py:1311
  212.3 9.8 %collective-permute-start.18 = (bf16[4,80,256]{2,1,0:T(8,128)(2,1)S(1)}, bf16[4,80,256]{2,1,0:T(8,128)(2,1)S(1)}, u32[]{:S(2)}, u32[]{:S(2)}) collective-permute-start(bf16[4,80,256]{2,1,0:T(8,128)(2,1)S(1)} %get-tuple-element.196), channel_id=1, source_target_pairs={{0,18},{1,19},{2,16},{3,17},{4,22},{5,23},{6,20},{7,21},{8,26},{9,... | collective-permute-start | bytes 491528 | tf_op jit(solution)/shard_map/ppermute | solution.py:1311
  212.7 9.8 %collective-permute-start.17 = (bf16[4,80,256]{2,1,0:T(8,128)(2,1)S(1)}, bf16[4,80,256]{2,1,0:T(8,128)(2,1)S(1)}, u32[]{:S(2)}, u32[]{:S(2)}) collective-permute-start(bf16[4,80,256]{2,1,0:T(8,128)(2,1)S(1)} %get-tuple-element.197), channel_id=1, source_target_pairs={{0,16},{1,17},{2,18},{3,19},{4,20},{5,21},{6,22},{7,23},{8,24},{9,... | collective-permute-start | bytes 491528 | tf_op jit(solution)/shard_map/ppermute | solution.py:1311
  214.2 8.2 %collective-permute-start.16 = (bf16[4,80,256]{2,1,0:T(8,128)(2,1)S(1)}, bf16[4,80,256]{2,1,0:T(8,128)(2,1)S(1)}, u32[]{:S(2)}, u32[]{:S(2)}) collective-permute-start(bf16[4,80,256]{2,1,0:T(8,128)(2,1)S(1)} %get-tuple-element.198), channel_id=1, source_target_pairs={{0,2},{1,3},{2,0},{3,1},{4,6},{5,7},{6,4},{7,5},{8,10},{9,11},{10,... | collective-permute-start | bytes 491528 | tf_op jit(solution)/shard_map/ppermute | solution.py:1311
  215.9 5.8 %collective-permute-start.20 = (bf16[1,160,256]{2,1,0:T(8,128)(2,1)S(1)}, bf16[1,160,256]{2,1,0:T(8,128)(2,1)S(1)}, u32[]{:S(2)}, u32[]{:S(2)}) collective-permute-start(bf16[1,160,256]{2,1,0:T(8,128)(2,1)S(1)} %get-tuple-element.200), channel_id=1, source_target_pairs={{0,8},{1,9},{2,10},{3,11},{4,12},{5,13},{6,14},{7,15},{8,0},{9,1},... | collective-permute-start | bytes 245768 | tf_op jit(solution)/shard_map/ppermute | solution.py:1311
  216.7 5.4 %collective-permute-start.19 = (bf16[1,160,256]{2,1,0:T(8,128)(2,1)S(1)}, bf16[1,160,256]{2,1,0:T(8,128)(2,1)S(1)}, u32[]{:S(2)}, u32[]{:S(2)}) collective-permute-start(bf16[1,160,256]{2,1,0:T(8,128)(2,1)S(1)} %get-tuple-element.201), channel_id=1, source_target_pairs={{0,4},{1,5},{2,6},{3,7},{4,0},{5,1},{6,2},{7,3},{8,12},{9,13},{10,... | collective-permute-start | bytes 245768 | tf_op jit(solution)/shard_map/ppermute | solution.py:1311
  224.3 6.0 %collective-permute-start.24 = (bf16[1,80,256]{2,1,0:T(8,128)(2,1)S(1)}, bf16[1,80,256]{2,1,0:T(8,128)(2,1)S(1)}, u32[]{:S(2)}, u32[]{:S(2)}) collective-permute-start(bf16[1,80,256]{2,1,0:T(8,128)(2,1)S(1)} %get-tuple-element.206), channel_id=1, source_target_pairs={{0,12},{1,13},{2,14},{3,15},{4,8},{5,9},{6,10},{7,11},{8,4},{9,5},... | collective-permute-start | bytes 122888 | tf_op jit(solution)/shard_map/ppermute | solution.py:1311
  225.9 5.2 %collective-permute-start.23 = (bf16[1,80,256]{2,1,0:T(8,128)(2,1)S(1)}, bf16[1,80,256]{2,1,0:T(8,128)(2,1)S(1)}, u32[]{:S(2)}, u32[]{:S(2)}) collective-permute-start(bf16[1,80,256]{2,1,0:T(8,128)(2,1)S(1)} %get-tuple-element.207), channel_id=1, source_target_pairs={{0,8},{1,9},{2,10},{3,11},{4,12},{5,13},{6,14},{7,15},{8,0},{9,1},... | collective-permute-start | bytes 122888 | tf_op jit(solution)/shard_map/ppermute | solution.py:1311
  226.4 4.7 %collective-permute-start.22 = (bf16[1,80,256]{2,1,0:T(8,128)(2,1)S(1)}, bf16[1,80,256]{2,1,0:T(8,128)(2,1)S(1)}, u32[]{:S(2)}, u32[]{:S(2)}) collective-permute-start(bf16[1,80,256]{2,1,0:T(8,128)(2,1)S(1)} %get-tuple-element.208), channel_id=1, source_target_pairs={{0,4},{1,5},{2,6},{3,7},{4,0},{5,1},{6,2},{7,3},{8,12},{9,13},{10,... | collective-permute-start | bytes 122888 | tf_op jit(solution)/shard_map/ppermute | solution.py:1311
  230.3 0.9 copy-start.5
  231.1 0.6 copy-start.6
  231.2 0.6 copy-start.7

commit v2 on v1

--- a/solution.py
+++ b/solution.py
@@ -375,7 +375,7 @@
             cc_ref[0, rows, :] = out_ref[...].astype(bf16)
             log_ref[0, image] = top_ref[...] * (scale * log2e) + jnp.log2(sum_ref[...])
 
-    @chunk_loop(ROWS, CHUNK)
+    @row_loop(ROWS, CHUNK)
     def _(start, rows):
         rows_ref[rows, :] = rows_in_ref[0, rows, :] + nn(cc_ref[0, rows, :], w_ref[0]) + bias_ref[...]
     for image in range(IMG_MAX):
@@ -492,6 +492,7 @@
     sum_ref[...] += nn(hidden_ref[FF_BLOCKS - 1], shrink(FF_BLOCKS - 1))
 
     head_weight = small_in_ref[0, :, 0:POS]
+    head_bias = nn(head_bias_ref[...], lanes_of(CLS + 4, 0))
     lane = lax.broadcasted_iota(jnp.int32, (1, POS), 1)
     is_box = (lane >= CLS) & (lane < CLS + 4)
     @chunk_loop(slots, STEP)
@@ -507,7 +508,7 @@
         box_one = one.astype(bf16)
         two, two_slope = gelu_parts(nn(box_one, box_ref[1]) + bias(8))
         box_two = two.astype(bf16)
-        box = jax.nn.sigmoid(nn(box_two, head_weight) + head_bias_ref[0:1, :])
+        box = jax.nn.sigmoid(nn(box_two, head_weight) + head_bias)
 
         head_cot = head_cot_ref[0, rows, :].astype(f32) * live
         grad_box = jnp.where(is_box, head_cot * box * (1.0 - box), 0.0).astype(bf16)
@@ -1438,8 +1439,7 @@
         early_held = stack(trade(early_held, bits, devices))
     early_parts = trade(early_held, groups[1], devices)
     bounds = run_of_images(segment, me)
-    head_row = jnp.pad(head_bias.astype(f32), (0, POS - CLS - 4))
-    head_row = jnp.broadcast_to(head_row[None], (8, POS))
+    head_row = head_bias[None]
     rest = jnp.zeros(logit_cotangent.shape[:2] + (POS - CLS - 4,), bf16)
     head_cotangent = jnp.concatenate([logit_cotangent, box_cotangent, rest], axis=-1)
     early_parts, bounds, head_row, head_cotangent, middle_held = lax.optimization_barrier(

time: 233 us -> 234 us (level)
  starting transfers between devices: 32 us -> 35.9 us
    ppermute x25, starting transfers between devices: 32 us -> 35.9 us  [swap(): return lax.ppermute(value, AXES, [(k, k ^ bits) for k in range(devices)])]
  transfers between devices with their start and end apart: 25 -> 25, of which waited for: 12 -> 10; matrix products, arithmetic and copies ran while one was open for 3% -> 3% of each run, Pallas kernels for 49% -> 48%
where the time goes in v2:
time: 234 us
  Pallas kernels  167 us (71%)
  starting transfers between devices  35.9 us (15%)
  waiting for transfers between devices  16.8 us (7%)
  local copies, waits for them, and re-layouts  8 us (3%)
  other arithmetic  5.29 us (2%)
    pallas_call x1, Pallas kernels, middle(): pl.pallas_call(functools.partial(middle_kernel, ordered), grid_spec=pltpu...  50.8 us
    ppermute x25, starting transfers between devices, swap(): return lax.ppermute(value, AXES, [(k, k ^ bits) for k in range(devices)])  35.9 us
    pallas_call x1, Pallas kernels, late_cross(): pl.pallas_call(late_cross_kernel, grid_spec=pltpu.PrefetchScalarGridSpec(...  34.7 us
    pallas_call x1, Pallas kernels, late_self(): pl.pallas_call(functools.partial(late_self_kernel, ordered), grid_spec=pl...  30.5 us
    pallas_call x1, Pallas kernels, early_cross(): pl.pallas_call(early_cross_kernel, grid_spec=pltpu.PrefetchScalarGridSpec...  24.4 us
    pallas_call x1, Pallas kernels, early_self(): pl.pallas_call(functools.partial(early_self_kernel, ordered), grid_spec=p...  23.7 us
    ppermute x25, waiting for transfers between devices, swap(): return lax.ppermute(value, AXES, [(k, k ^ bits) for k in range(devices)])  16.8 us
  transfers between devices with their start and end apart: 25, of which 10 were waited for; matrix products, arithmetic and copies ran while one was open for 3% of the time, Pallas kernels for 48%

profile of v2, /device:TPU:0, one launch (start us, length us, event | category | flops | bytes accessed | tf_op | source)
XLA Modules:
  0.0 234.4 jit_solution(11010586497094206835)
XLA Ops:
  0.7 1.7 pack.1
  2.4 5.0 %collective-permute-start.2 = (bf16[1,240,256]{2,1,0:T(8,128)(2,1)}, bf16[1,240,256]{2,1,0:T(8,128)(2,1)S(1)}, u32[]{:S(2)}, u32[]{:S(2)}) collective-permute-start(bf16[1,240,256]{2,1,0:T(8,128)(2,1)} %bitcast.20), channel_id=1, source_target_pairs={{0,12},{1,13},{2,14},{3,15},{4,8},{5,9},{6,10},{7,11},{8,4},{9,5},... | collective-permute-start | bytes 368648 | tf_op jit(solution)/shard_map/ppermute | solution.py:1312
  7.5 0.6 collective-permute-start
  8.0 0.8 fusion.4
  8.9 0.9 convert_reduce_fusion
  9.8 0.1 pad.12.clone
  9.8 0.6 select_select_fusion.bounds
  10.5 1.4 collective-permute-done.2
  11.9 6.1 %collective-permute-done.1 = bf16[1,240,256]{2,1,0:T(8,128)(2,1)S(1)} collective-permute-done((bf16[1,240,256]{2,1,0:T(8,128)(2,1)}, bf16[1,240,256]{2,1,0:T(8,128)(2,1)S(1)}, u32[]{:S(2)}, u32[]{:S(2)}) %collective-permute-start.1) | collective-permute-done | bytes 122912 | tf_op jit(solution)/shard_map/ppermute | solution.py:1312
  18.0 0.8 slice.105
  18.9 2.5 %collective-permute-start.5 = (bf16[4,80,256]{2,1,0:T(8,128)(2,1)S(1)}, bf16[4,80,256]{2,1,0:T(8,128)(2,1)S(1)}, u32[]{:S(2)}, u32[]{:S(2)}) collective-permute-start(bf16[4,80,256]{2,1,0:T(8,128)(2,1)S(1)} %pad_maximum_fusion.2), channel_id=1, source_target_pairs={{0,18},{1,19},{2,16},{3,17},{4,22},{5,23},{6,20},{7,21},{8,26},{9,... | collective-permute-start | bytes 491528 | tf_op jit(solution)/shard_map/ppermute | solution.py:1312
  21.4 0.5 collective-permute-start.4
  21.9 0.5 collective-permute-start.3
  22.4 1.6 copy.36
  24.1 0.0 copy-start.3
  24.1 0.4 copy.37
  24.5 1.2 maximum_maximum_fusion.head_cot_ref
  25.8 0.5 collective-permute-done.5
  26.3 2.3 collective-permute-done.4
  28.6 0.1 collective-permute-done.3
  28.7 0.0 copy-start.4
  28.8 0.1 collective-permute-start.6
  28.8 1.8 collective-permute-start.9
  30.6 1.3 collective-permute-start.8
  31.9 0.5 collective-permute-start.7
  32.4 0.8 copy-done.10
  33.2 23.7 %early_self.1 = (f32[2,1536,256]{2,1,0:T(8,128)}, bf16[2,1536,256]{2,1,0:T(8,128)(2,1)}, bf16[2,1536,256]{2,1,0:T(8,128)(2,1)}, bf16[2,1536,256]{2,1,0:T(8,128)(...) custom-call(s32[2,16]{1,0:T(2,128)} %select_select_fusion.bounds, ...), custom_call_target="tpu_custom_call" | custom-call | flops 16000000000 | bytes 18000000 | tf_op jit(solution)/shard_map/early_self/pallas_call | solution.py:935
  56.9 0.2 pad_maximum_fusion.mine_ref
  57.1 0.1 collective-permute-start.10
  57.2 24.4 %early_cross.1 = (f32[2,1200,256]{2,1,0:T(8,128)}, bf16[2,1536,256]{2,1,0:T(8,128)(2,1)}, f32[2,12,1,1024]{3,2,1,0:T(1,128)}) custom-call(s32[2,16]{1,0:T(2,128)} %select_select_fusion.bounds, f32[2,1536,256]{2,1,0:T(8,128)} %get-tuple-element.111.rows_in_ref, bf16[2,1536,256]{2,1,0:T(8,128)(2,1)} %get-tuple-element.119.cq_ref, ...), custom_call_target="tpu_custom_call" | custom-call | flops 16000000000 | bytes 14000000 | tf_op jit(solution)/shard_map/early_cross/pallas_call | solution.py:976
  81.6 0.0 copy-start.9
  81.6 1.0 copy-done.9
  82.6 50.8 %middle.1 = (bf16[2,1200,256]{2,1,0:T(8,128)(2,1)}, f32[2,1200,256]{2,1,0:T(8,128)}, f32[16,160,256]{2,1,0:T(8,128)}, bf16[16,160,256]{2,1,0:T(8,128)(2,1)}, f32[256,128]{1,0:T(8,128)}, /*index=5*/f32[32,256]{1,0:T(8,128)}) custom-call(s32[2,16]{1,0:T(2,128)} %select_select_fusion.bounds, f32[2,1200,256]{2,1,0:T(8,128)} %get-tuple-element.124.x_ref, ...), custom_call_target="tpu_custom_call" | custom-call | flops 20000000000 | bytes 18000000 | tf_op jit(solution)/shard_map/middle/pallas_call | solution.py:1017
  133.4 1.8 collective-permute-start.11
  135.2 34.7 %late_cross.1 = (bf16[2,1536,256]{2,1,0:T(8,128)(2,1)}, f32[2,2048,256]{2,1,0:T(8,128)}, f32[3,256,256]{2,1,0:T(8,128)}, f32[8,256]{1,0:T(8,128)}) custom-call(s32[2,16]{1,0:T(2,128)} %select_select_fusion.bounds, f32[2,1200,256]{2,1,0:T(8,128)} %get-tuple-element.132.grad_ref, bf16[2,2048,256]{2,1,0:T(8,128)(2,1)} %memory_ref.3, ...), custom_call_target="tpu_custom_call" | custom-call | flops 24000000000 | bytes 18000000 | tf_op jit(solution)/shard_map/late_cross/pallas_call | solution.py:1065
  169.9 0.4 fusion.9
  170.4 0.1 fusion.10
  170.5 0.6 collective-permute-start.12
  171.1 5.4 %collective-permute-start.13 = (bf16[4,160,256]{2,1,0:T(8,128)(2,1)S(1)}, bf16[4,160,256]{2,1,0:T(8,128)(2,1)S(1)}, u32[]{:S(2)}, u32[]{:S(2)}) collective-permute-start(bf16[4,160,256]{2,1,0:T(8,128)(2,1)S(1)} %get-tuple-element.156), channel_id=1, source_target_pairs={{0,16},{1,17},{2,18},{3,19},{4,20},{5,21},{6,22},{7,23},{8,24},{9,... | collective-permute-start | bytes 983048 | tf_op jit(solution)/shard_map/ppermute | solution.py:1312
  176.5 30.5 %late_self.1 = (f32[2,1200,256]{2,1,0:T(8,128)}, f32[16,80,256]{2,1,0:T(8,128)}, bf16[16,80,256]{2,1,0:T(8,128)(2,1)}) custom-call(s32[2,16]{1,0:T(2,128)} %select_select_fusion.bounds, f32[2,1200,256]{2,1,0:T(8,128)} %get-tuple-element.132.grad_ref, bf16[2,1536,256]{2,1,0:T(8,128)(2,1)} %get-tuple-element.140.gcq_ref, bf16[2,1200,256]{2,1,0:T(8,128)(2,1)} %target_ref.3, ...), custom_call_target="tpu_custom_call" | custom-call | flops 20000000000 | bytes 14000000 | tf_op jit(solution)/shard_map/late_self/pallas_call | solution.py:1110
  207.0 0.1 collective-permute-start.15
  207.1 0.2 fusion.7
  207.3 4.6 %collective-permute-start.21 = (bf16[1,160,256]{2,1,0:T(8,128)(2,1)S(1)}, bf16[1,160,256]{2,1,0:T(8,128)(2,1)S(1)}, u32[]{:S(2)}, u32[]{:S(2)}) collective-permute-start(bf16[1,160,256]{2,1,0:T(8,128)(2,1)S(1)} %get-tuple-element.199), channel_id=1, source_target_pairs={{0,12},{1,13},{2,14},{3,15},{4,8},{5,9},{6,10},{7,11},{8,4},{9,5},... | collective-permute-start | bytes 245768 | tf_op jit(solution)/shard_map/ppermute | solution.py:1312
  211.8 0.2 fusion.8
  212.1 3.0 %collective-permute-start.18 = (bf16[4,80,256]{2,1,0:T(8,128)(2,1)S(1)}, bf16[4,80,256]{2,1,0:T(8,128)(2,1)S(1)}, u32[]{:S(2)}, u32[]{:S(2)}) collective-permute-start(bf16[4,80,256]{2,1,0:T(8,128)(2,1)S(1)} %get-tuple-element.196), channel_id=1, source_target_pairs={{0,18},{1,19},{2,16},{3,17},{4,22},{5,23},{6,20},{7,21},{8,26},{9,... | collective-permute-start | bytes 491528 | tf_op jit(solution)/shard_map/ppermute | solution.py:1312
  215.0 0.6 collective-permute-start.16
  215.7 2.6 %collective-permute-start.19 = (bf16[1,160,256]{2,1,0:T(8,128)(2,1)S(1)}, bf16[1,160,256]{2,1,0:T(8,128)(2,1)S(1)}, u32[]{:S(2)}, u32[]{:S(2)}) collective-permute-start(bf16[1,160,256]{2,1,0:T(8,128)(2,1)S(1)} %get-tuple-element.201), channel_id=1, source_target_pairs={{0,4},{1,5},{2,6},{3,7},{4,0},{5,1},{6,2},{7,3},{8,12},{9,13},{10,... | collective-permute-start | bytes 245768 | tf_op jit(solution)/shard_map/ppermute | solution.py:1312
  218.3 3.4 %collective-permute-done.20 = bf16[1,160,256]{2,1,0:T(8,128)(2,1)S(1)} collective-permute-done((bf16[1,160,256]{2,1,0:T(8,128)(2,1)S(1)}, bf16[1,160,256]{2,1,0:T(8,128)(2,1)S(1)}, u32[]{:S(2)}, u32[]{:S(2)}) %collective-permute-start.20) | collective-permute-done | bytes 81952 | tf_op jit(solution)/shard_map/ppermute | solution.py:1312
  221.7 0.5 collective-permute-done.19
  222.2 0.9 collective-permute-done.17
  223.2 0.5 slice_bitcast_fusion.3
  223.7 0.5 slice_bitcast_fusion.2
  224.2 0.7 slice_bitcast_fusion
  224.9 0.1 fusion.5
  225.0 2.0 collective-permute-start.24
  227.0 2.4 %collective-permute-start.22 = (bf16[1,80,256]{2,1,0:T(8,128)(2,1)S(1)}, bf16[1,80,256]{2,1,0:T(8,128)(2,1)S(1)}, u32[]{:S(2)}, u32[]{:S(2)}) collective-permute-start(bf16[1,80,256]{2,1,0:T(8,128)(2,1)S(1)} %get-tuple-element.208), channel_id=1, source_target_pairs={{0,4},{1,5},{2,6},{3,7},{4,0},{5,1},{6,2},{7,3},{8,12},{9,13},{10,... | collective-permute-start | bytes 122888 | tf_op jit(solution)/shard_map/ppermute | solution.py:1312
  229.4 0.6 pad_maximum_fusion.3
  230.0 0.6 slice.146.keep
  230.7 0.2 collective-permute-done.24.refs_2_
  230.8 1.3 collective-permute-done.23.refs_1_
  232.1 0.0 collective-permute-done.22.refs_0_
  232.2 0.6 copy-done.6
  232.7 0.0 copy-done.7
  232.8 1.6 finish.1
  (55 shorter events, 0.4 us)
Async XLA Ops:
  0.7 23.4 %copy-start.8 = (bf16[2,1200,4]{1,2,0:T(4,128)(2,1)S(1)}, bf16[2,1200,4]{1,2,0:T(4,128)(2,1)}, u32[]{:S(2)}) copy-start(bf16[2,1200,4]{1,2,0:T(4,128)(2,1)} %param.37) | copy-start | bytes 57604
  2.4 9.5 %collective-permute-start.2 = (bf16[1,240,256]{2,1,0:T(8,128)(2,1)}, bf16[1,240,256]{2,1,0:T(8,128)(2,1)S(1)}, u32[]{:S(2)}, u32[]{:S(2)}) collective-permute-start(bf16[1,240,256]{2,1,0:T(8,128)(2,1)} %bitcast.20), channel_id=1, source_target_pairs={{0,12},{1,13},{2,14},{3,15},{4,8},{5,9},{6,10},{7,11},{8,4},{9,5},... | collective-permute-start | bytes 368648 | tf_op jit(solution)/shard_map/ppermute | solution.py:1312
  7.4 10.6 %collective-permute-start.1 = (bf16[1,240,256]{2,1,0:T(8,128)(2,1)}, bf16[1,240,256]{2,1,0:T(8,128)(2,1)S(1)}, u32[]{:S(2)}, u32[]{:S(2)}) collective-permute-start(bf16[1,240,256]{2,1,0:T(8,128)(2,1)} %bitcast.21), channel_id=1, source_target_pairs={{0,8},{1,9},{2,10},{3,11},{4,12},{5,13},{6,14},{7,15},{8,0},{9,1},... | collective-permute-start | bytes 368648 | tf_op jit(solution)/shard_map/ppermute | solution.py:1312
  7.5 10.6 %collective-permute-start = (bf16[1,240,256]{2,1,0:T(8,128)(2,1)}, bf16[1,240,256]{2,1,0:T(8,128)(2,1)S(1)}, u32[]{:S(2)}, u32[]{:S(2)}) collective-permute-start(bf16[1,240,256]{2,1,0:T(8,128)(2,1)} %bitcast.22), channel_id=1, source_target_pairs={{0,4},{1,5},{2,6},{3,7},{4,0},{5,1},{6,2},{7,3},{8,12},{9,13},{10,... | collective-permute-start | bytes 368648 | tf_op jit(solution)/shard_map/ppermute | solution.py:1312
  18.9 7.5 %collective-permute-start.5 = (bf16[4,80,256]{2,1,0:T(8,128)(2,1)S(1)}, bf16[4,80,256]{2,1,0:T(8,128)(2,1)S(1)}, u32[]{:S(2)}, u32[]{:S(2)}) collective-permute-start(bf16[4,80,256]{2,1,0:T(8,128)(2,1)S(1)} %pad_maximum_fusion.2), channel_id=1, source_target_pairs={{0,18},{1,19},{2,16},{3,17},{4,22},{5,23},{6,20},{7,21},{8,26},{9,... | collective-permute-start | bytes 491528 | tf_op jit(solution)/shard_map/ppermute | solution.py:1312
  21.4 7.2 %collective-permute-start.4 = (bf16[4,80,256]{2,1,0:T(8,128)(2,1)S(1)}, bf16[4,80,256]{2,1,0:T(8,128)(2,1)S(1)}, u32[]{:S(2)}, u32[]{:S(2)}) collective-permute-start(bf16[4,80,256]{2,1,0:T(8,128)(2,1)S(1)} %pad_maximum_fusion.2), channel_id=1, source_target_pairs={{0,16},{1,17},{2,18},{3,19},{4,20},{5,21},{6,22},{7,23},{8,24},{9,... | collective-permute-start | bytes 491528 | tf_op jit(solution)/shard_map/ppermute | solution.py:1312
  21.9 6.8 %collective-permute-start.3 = (bf16[4,80,256]{2,1,0:T(8,128)(2,1)S(1)}, bf16[4,80,256]{2,1,0:T(8,128)(2,1)S(1)}, u32[]{:S(2)}, u32[]{:S(2)}) collective-permute-start(bf16[4,80,256]{2,1,0:T(8,128)(2,1)S(1)} %pad_maximum_fusion.2), channel_id=1, source_target_pairs={{0,2},{1,3},{2,0},{3,1},{4,6},{5,7},{6,4},{7,5},{8,10},{9,11},{10,... | collective-permute-start | bytes 491528 | tf_op jit(solution)/shard_map/ppermute | solution.py:1312
  24.1 1.6 copy-start.3
  28.7 3.7 %copy-start.4 = (bf16[16,80,256]{2,1,0:T(8,128)(2,1)}, bf16[16,80,256]{2,1,0:T(8,128)(2,1)S(1)}, u32[]{:S(2)}) copy-start(bf16[16,80,256]{2,1,0:T(8,128)(2,1)S(1)} %constant_dynamic-update-slice_fusion.mine_ref) | copy-start | bytes 1966084
  28.8 3.6 %collective-permute-start.6 = (bf16[16,80,256]{2,1,0:T(8,128)(2,1)S(1)}, bf16[16,80,256]{2,1,0:T(8,128)(2,1)S(1)}, u32[]{:S(2)}, u32[]{:S(2)}) collective-permute-start(bf16[16,80,256]{2,1,0:T(8,128)(2,1)S(1)} %constant_dynamic-update-slice_fusion.mine_ref), channel_id=1, source_target_pairs={{0,1},{1,0},{2,3},{3,2},{4,5},{5,4},{6,7},{7,6},{8,9},{9,8},{10,11... | collective-permute-start | bytes 1966088 | tf_op jit(solution)/shard_map/ppermute | solution.py:1312
  28.8 28.1 %collective-permute-start.9 = (bf16[4,160,256]{2,1,0:T(8,128)(2,1)S(1)}, bf16[4,160,256]{2,1,0:T(8,128)(2,1)S(1)}, u32[]{:S(2)}, u32[]{:S(2)}) collective-permute-start(bf16[4,160,256]{2,1,0:T(8,128)(2,1)S(1)} %pad_maximum_fusion.1), channel_id=1, source_target_pairs={{0,18},{1,19},{2,16},{3,17},{4,22},{5,23},{6,20},{7,21},{8,26},{9,... | collective-permute-start | bytes 983048 | tf_op jit(solution)/shard_map/ppermute | solution.py:1312
  30.6 26.3 %collective-permute-start.8 = (bf16[4,160,256]{2,1,0:T(8,128)(2,1)S(1)}, bf16[4,160,256]{2,1,0:T(8,128)(2,1)S(1)}, u32[]{:S(2)}, u32[]{:S(2)}) collective-permute-start(bf16[4,160,256]{2,1,0:T(8,128)(2,1)S(1)} %pad_maximum_fusion.1), channel_id=1, source_target_pairs={{0,16},{1,17},{2,18},{3,19},{4,20},{5,21},{6,22},{7,23},{8,24},{9,... | collective-permute-start | bytes 983048 | tf_op jit(solution)/shard_map/ppermute | solution.py:1312
  31.9 25.0 %collective-permute-start.7 = (bf16[4,160,256]{2,1,0:T(8,128)(2,1)S(1)}, bf16[4,160,256]{2,1,0:T(8,128)(2,1)S(1)}, u32[]{:S(2)}, u32[]{:S(2)}) collective-permute-start(bf16[4,160,256]{2,1,0:T(8,128)(2,1)S(1)} %pad_maximum_fusion.1), channel_id=1, source_target_pairs={{0,2},{1,3},{2,0},{3,1},{4,6},{5,7},{6,4},{7,5},{8,10},{9,11},{10,... | collective-permute-start | bytes 983048 | tf_op jit(solution)/shard_map/ppermute | solution.py:1312
  32.4 0.8 copy-start.10
  57.1 24.4 %copy-start.1 = (bf16[16,160,256]{2,1,0:T(8,128)(2,1)}, bf16[16,160,256]{2,1,0:T(8,128)(2,1)S(1)}, u32[]{:S(2)}) copy-start(bf16[16,160,256]{2,1,0:T(8,128)(2,1)S(1)} %pad_maximum_fusion.mine_ref) | copy-start | bytes 3932164
  57.1 24.4 %collective-permute-start.10 = (bf16[16,160,256]{2,1,0:T(8,128)(2,1)S(1)}, bf16[16,160,256]{2,1,0:T(8,128)(2,1)S(1)}, u32[]{:S(2)}, u32[]{:S(2)}) collective-permute-start(bf16[16,160,256]{2,1,0:T(8,128)(2,1)S(1)} %pad_maximum_fusion.mine_ref), channel_id=1, source_target_pairs={{0,1},{1,0},{2,3},{3,2},{4,5},{5,4},{6,7},{7,6},{8,9},{9,8},{10,11... | collective-permute-start | bytes 3932168 | tf_op jit(solution)/shard_map/ppermute | solution.py:1312
  81.6 1.1 copy-start.9
  133.4 36.5 %collective-permute-start.11 = (bf16[16,160,256]{2,1,0:T(8,128)(2,1)}, bf16[16,160,256]{2,1,0:T(8,128)(2,1)S(1)}, u32[]{:S(2)}, u32[]{:S(2)}) collective-permute-start(bf16[16,160,256]{2,1,0:T(8,128)(2,1)} %get-tuple-element.136), channel_id=1, source_target_pairs={{0,1},{1,0},{2,3},{3,2},{4,5},{5,4},{6,7},{7,6},{8,9},{9,8},{10,11... | collective-permute-start | bytes 3932168 | tf_op jit(solution)/shard_map/ppermute | solution.py:1312
  135.2 34.7 %copy-start = (f32[16,160,256]{2,1,0:T(8,128)S(1)}, f32[16,160,256]{2,1,0:T(8,128)}, u32[]{:S(2)}) copy-start(f32[16,160,256]{2,1,0:T(8,128)} %get-tuple-element.138) | copy-start | bytes 7864324
  170.5 36.5 %collective-permute-start.12 = (bf16[4,160,256]{2,1,0:T(8,128)(2,1)S(1)}, bf16[4,160,256]{2,1,0:T(8,128)(2,1)S(1)}, u32[]{:S(2)}, u32[]{:S(2)}) collective-permute-start(bf16[4,160,256]{2,1,0:T(8,128)(2,1)S(1)} %get-tuple-element.155), channel_id=1, source_target_pairs={{0,2},{1,3},{2,0},{3,1},{4,6},{5,7},{6,4},{7,5},{8,10},{9,11},{10,... | collective-permute-start | bytes 983048 | tf_op jit(solution)/shard_map/ppermute | solution.py:1312
  171.1 35.9 %collective-permute-start.13 = (bf16[4,160,256]{2,1,0:T(8,128)(2,1)S(1)}, bf16[4,160,256]{2,1,0:T(8,128)(2,1)S(1)}, u32[]{:S(2)}, u32[]{:S(2)}) collective-permute-start(bf16[4,160,256]{2,1,0:T(8,128)(2,1)S(1)} %get-tuple-element.156), channel_id=1, source_target_pairs={{0,16},{1,17},{2,18},{3,19},{4,20},{5,21},{6,22},{7,23},{8,24},{9,... | collective-permute-start | bytes 983048 | tf_op jit(solution)/shard_map/ppermute | solution.py:1312
  176.5 30.5 %collective-permute-start.14 = (bf16[4,160,256]{2,1,0:T(8,128)(2,1)S(1)}, bf16[4,160,256]{2,1,0:T(8,128)(2,1)S(1)}, u32[]{:S(2)}, u32[]{:S(2)}) collective-permute-start(bf16[4,160,256]{2,1,0:T(8,128)(2,1)S(1)} %get-tuple-element.157), channel_id=1, source_target_pairs={{0,18},{1,19},{2,16},{3,17},{4,22},{5,23},{6,20},{7,21},{8,26},{9,... | collective-permute-start | bytes 983048 | tf_op jit(solution)/shard_map/ppermute | solution.py:1312
  207.0 4.9 %copy-start.2 = (f32[16,80,256]{2,1,0:T(8,128)S(1)}, f32[16,80,256]{2,1,0:T(8,128)}, u32[]{:S(2)}) copy-start(f32[16,80,256]{2,1,0:T(8,128)} %get-tuple-element.158) | copy-start | bytes 3932164
  207.0 4.8 %collective-permute-start.15 = (bf16[16,80,256]{2,1,0:T(8,128)(2,1)}, bf16[16,80,256]{2,1,0:T(8,128)(2,1)S(1)}, u32[]{:S(2)}, u32[]{:S(2)}) collective-permute-start(bf16[16,80,256]{2,1,0:T(8,128)(2,1)} %get-tuple-element.159), channel_id=1, source_target_pairs={{0,1},{1,0},{2,3},{3,2},{4,5},{5,4},{6,7},{7,6},{8,9},{9,8},{10,11... | collective-permute-start | bytes 1966088 | tf_op jit(solution)/shard_map/ppermute | solution.py:1312
  207.3 8.4 %collective-permute-start.21 = (bf16[1,160,256]{2,1,0:T(8,128)(2,1)S(1)}, bf16[1,160,256]{2,1,0:T(8,128)(2,1)S(1)}, u32[]{:S(2)}, u32[]{:S(2)}) collective-permute-start(bf16[1,160,256]{2,1,0:T(8,128)(2,1)S(1)} %get-tuple-element.199), channel_id=1, source_target_pairs={{0,12},{1,13},{2,14},{3,15},{4,8},{5,9},{6,10},{7,11},{8,4},{9,5},... | collective-permute-start | bytes 245768 | tf_op jit(solution)/shard_map/ppermute | solution.py:1312
  212.1 10.1 %collective-permute-start.18 = (bf16[4,80,256]{2,1,0:T(8,128)(2,1)S(1)}, bf16[4,80,256]{2,1,0:T(8,128)(2,1)S(1)}, u32[]{:S(2)}, u32[]{:S(2)}) collective-permute-start(bf16[4,80,256]{2,1,0:T(8,128)(2,1)S(1)} %get-tuple-element.196), channel_id=1, source_target_pairs={{0,18},{1,19},{2,16},{3,17},{4,22},{5,23},{6,20},{7,21},{8,26},{9,... | collective-permute-start | bytes 491528 | tf_op jit(solution)/shard_map/ppermute | solution.py:1312
  215.0 8.1 %collective-permute-start.17 = (bf16[4,80,256]{2,1,0:T(8,128)(2,1)S(1)}, bf16[4,80,256]{2,1,0:T(8,128)(2,1)S(1)}, u32[]{:S(2)}, u32[]{:S(2)}) collective-permute-start(bf16[4,80,256]{2,1,0:T(8,128)(2,1)S(1)} %get-tuple-element.197), channel_id=1, source_target_pairs={{0,16},{1,17},{2,18},{3,19},{4,20},{5,21},{6,22},{7,23},{8,24},{9,... | collective-permute-start | bytes 491528 | tf_op jit(solution)/shard_map/ppermute | solution.py:1312
  215.0 8.1 %collective-permute-start.16 = (bf16[4,80,256]{2,1,0:T(8,128)(2,1)S(1)}, bf16[4,80,256]{2,1,0:T(8,128)(2,1)S(1)}, u32[]{:S(2)}, u32[]{:S(2)}) collective-permute-start(bf16[4,80,256]{2,1,0:T(8,128)(2,1)S(1)} %get-tuple-element.198), channel_id=1, source_target_pairs={{0,2},{1,3},{2,0},{3,1},{4,6},{5,7},{6,4},{7,5},{8,10},{9,11},{10,... | collective-permute-start | bytes 491528 | tf_op jit(solution)/shard_map/ppermute | solution.py:1312
  215.7 6.0 %collective-permute-start.20 = (bf16[1,160,256]{2,1,0:T(8,128)(2,1)S(1)}, bf16[1,160,256]{2,1,0:T(8,128)(2,1)S(1)}, u32[]{:S(2)}, u32[]{:S(2)}) collective-permute-start(bf16[1,160,256]{2,1,0:T(8,128)(2,1)S(1)} %get-tuple-element.200), channel_id=1, source_target_pairs={{0,8},{1,9},{2,10},{3,11},{4,12},{5,13},{6,14},{7,15},{8,0},{9,1},... | collective-permute-start | bytes 245768 | tf_op jit(solution)/shard_map/ppermute | solution.py:1312
  215.7 6.5 %collective-permute-start.19 = (bf16[1,160,256]{2,1,0:T(8,128)(2,1)S(1)}, bf16[1,160,256]{2,1,0:T(8,128)(2,1)S(1)}, u32[]{:S(2)}, u32[]{:S(2)}) collective-permute-start(bf16[1,160,256]{2,1,0:T(8,128)(2,1)S(1)} %get-tuple-element.201), channel_id=1, source_target_pairs={{0,4},{1,5},{2,6},{3,7},{4,0},{5,1},{6,2},{7,3},{8,12},{9,13},{10,... | collective-permute-start | bytes 245768 | tf_op jit(solution)/shard_map/ppermute | solution.py:1312
  225.0 5.9 %collective-permute-start.24 = (bf16[1,80,256]{2,1,0:T(8,128)(2,1)S(1)}, bf16[1,80,256]{2,1,0:T(8,128)(2,1)S(1)}, u32[]{:S(2)}, u32[]{:S(2)}) collective-permute-start(bf16[1,80,256]{2,1,0:T(8,128)(2,1)S(1)} %get-tuple-element.206), channel_id=1, source_target_pairs={{0,12},{1,13},{2,14},{3,15},{4,8},{5,9},{6,10},{7,11},{8,4},{9,5},... | collective-permute-start | bytes 122888 | tf_op jit(solution)/shard_map/ppermute | solution.py:1312
  227.0 5.1 %collective-permute-start.23 = (bf16[1,80,256]{2,1,0:T(8,128)(2,1)S(1)}, bf16[1,80,256]{2,1,0:T(8,128)(2,1)S(1)}, u32[]{:S(2)}, u32[]{:S(2)}) collective-permute-start(bf16[1,80,256]{2,1,0:T(8,128)(2,1)S(1)} %get-tuple-element.207), channel_id=1, source_target_pairs={{0,8},{1,9},{2,10},{3,11},{4,12},{5,13},{6,14},{7,15},{8,0},{9,1},... | collective-permute-start | bytes 122888 | tf_op jit(solution)/shard_map/ppermute | solution.py:1312
  227.0 5.2 %collective-permute-start.22 = (bf16[1,80,256]{2,1,0:T(8,128)(2,1)S(1)}, bf16[1,80,256]{2,1,0:T(8,128)(2,1)S(1)}, u32[]{:S(2)}, u32[]{:S(2)}) collective-permute-start(bf16[1,80,256]{2,1,0:T(8,128)(2,1)S(1)} %get-tuple-element.208), channel_id=1, source_target_pairs={{0,4},{1,5},{2,6},{3,7},{4,0},{5,1},{6,2},{7,3},{8,12},{9,13},{10,... | collective-permute-start | bytes 122888 | tf_op jit(solution)/shard_map/ppermute | solution.py:1312
  230.8 1.3 copy-start.5
  232.1 0.6 copy-start.6
  232.2 0.6 copy-start.7
